TPU v7x, 32 devices: a whole 2x2x4 slice. The times are simulated.
32 devices in a mesh: section: 4 (over x, core), seq: 4 (over z), head: 2 (over y).
Axes of the slice: x: 2, y: 2, z: 4, core: 2. Of those that a mesh axis runs over, the one named last changes fastest.
Arguments:
- queries: bfloat16 [4, 512, 1536], P('section', 'seq', 'head'), may hold values from -240 to 240
- grad_out: bfloat16 [4, 512, 1536], P('section', 'seq', 'head'), may hold values from -96 to 96
- keys: bfloat16 [4, 256, 768], P('section', 'seq', 'head'), may hold values from -6 to 6
- values: bfloat16 [4, 256, 768], P('section', 'seq', 'head'), may hold values from -6 to 6
- proj_query: bfloat16 [4, 5376, 1536], P('section', None, 'head'), may hold values from -0.15625 to 0.15625
- section_span: int32 [4], replicated, may hold values from 0 to 3, each once
- span_prefix: int32 [4], replicated, may hold values from 128 to 256, as said below
Outputs:
- grad_input: bfloat16 [4, 5376, 512], P('section', 'head', 'seq')
- grad_key: bfloat16 [4, 256, 768], P('section', 'seq', 'head')
- grad_value: bfloat16 [4, 256, 768], P('section', 'seq', 'head')
Inputs may be any that keep to these rules, and one draw needn't show every extreme that they name: `span_prefix`: some entry equals 256 in every draw.
All inputs are finite; a program needn't handle non-finite values.
Results may differ from a plain program's by a relative error of at most 0.023.
Values may be sent and summed in bfloat16 or wider, within the bound.
No kernel may reach another device: no remote copies, remote signals or barrier semaphores. Data moves between devices by JAX's collectives and lax.ppermute only.
A program may use at most 64 MiB of HBM per device.

v0:
```python
import functools
import math

import jax
import jax.numpy as jnp
from jax import lax
from jax.experimental import pallas as pl
from jax.experimental.pallas import tpu as pltpu
from jax.sharding import PartitionSpec as P

HD = 128
MOST_PARTNERS = 4
VMEM_LIMIT = 40 * 1024 * 1024

query_scale = 168.0 ** (-0.5)
exp2_scale = query_scale * math.log2(math.e)


def shifted(block, axis, distance):
    devices = range(lax.axis_size(axis))
    route = [((i - distance) % len(devices), i) for i in devices]
    return lax.ppermute(block, axis, route)


def swapped(block, axis, distance):
    return lax.ppermute(block, axis, [(i, i ^ distance) for i in range(lax.axis_size(axis))])


def dot(left, right, left_dim, right_dim):
    return lax.dot_general(
        left, right, (((left_dim,), (right_dim,)), ((), ())), preferred_element_type=jnp.float32
    )


def in_hbm(x):
    return pltpu.with_memory_space_constraint(x, pltpu.HBM)


def join_kernel(n_copies, key_ref, value_ref, grad_ref, *refs):
    *outs, grad_low, grad_high, sems = refs
    width, rows = key_ref.shape[2], grad_low.shape[0]
    pairs = [
        (key_ref.at[0], outs[0].at[:, :width]),
        (value_ref.at[0], outs[0].at[:, width:]),
        (grad_ref.at[0, :rows, :], grad_low),
        (grad_ref.at[0, rows:, :], grad_high),
    ]
    copies = [pltpu.make_async_copy(a, b, sems.at[i]) for i, (a, b) in enumerate(pairs)]
    for copy in copies:
        copy.start()
    for copy in copies[:2]:
        copy.wait()
    for out in outs[1:]:
        out[...] = outs[0][...]
    for copy in copies[2:]:
        copy.wait()


def stage_kernel(n_head, span_ref, prefix_ref, q_ref, w_ref, limit_out, q_out, *refs):
    *other_outs, span, prefix, sems, small_sems = refs
    feats = w_ref.shape[1] // n_head
    head = lax.axis_index("head")
    copies = []
    for r, out in enumerate(other_outs):
        start = pl.multiple_of(lax.rem(head + r + 1, n_head) * feats, 16)
        copies.append((w_ref.at[0, pl.ds(start, feats), :], out))
    copies.append((q_ref.at[0], q_out))
    copies = [pltpu.make_async_copy(a, b, sems.at[i]) for i, (a, b) in enumerate(copies)]
    small = [
        pltpu.make_async_copy(a, b, small_sems.at[i])
        for i, (a, b) in enumerate([(span_ref, span), (prefix_ref, prefix)])
    ]
    for copy in small + copies:
        copy.start()
    for copy in small:
        copy.wait()
    live = prefix[span[lax.axis_index("section")]]
    limit_out[...] = jnp.full(limit_out.shape, live, jnp.int32)
    for copy in copies:
        copy.wait()


def pair_of(refs, g):
    cols = [slice((2 * g + i) * HD, (2 * g + i + 1) * HD) for i in range(2)]
    return jnp.concatenate([ref[:, c] for c in cols for ref in refs], axis=0)


def cols_of(g, start=0):
    return slice(start + g * HD, start + (g + 1) * HD)


def attention_kernel(partners, n_other, limit_ref, q_ref, *refs):
    n_blocks = 1 + len(partners)
    kv_refs = refs[:n_blocks]
    d_low, d_high, *refs = refs[n_blocks:]
    w_refs = refs[:n_other]
    grad_ref, probs_ref, dscores_ref, *part_refs = refs[n_other:]

    held, both = kv_refs[0].shape
    width = both // 2
    seq = lax.axis_index("seq")
    spots = []
    for r in [0, *partners]:
        first = jnp.bitwise_xor(seq, r) * held if partners else 0
        spots.append(first + lax.broadcasted_iota(jnp.int32, (held, 1), 0))
    alive = jnp.concatenate(spots, axis=0) < limit_ref[0:1, 0:1]

    rows = q_ref.shape[0]
    groups = range(width // HD)
    keys = [jnp.concatenate([ref[:, cols_of(g)] for ref in kv_refs], axis=0) for g in groups]
    scores = [dot(keys[g], pair_of((q_ref,), g), 1, 1) for g in groups]
    dprobs = []
    for g in groups:
        value = jnp.concatenate([ref[:, cols_of(g, width)] for ref in kv_refs], axis=0)
        dprobs.append(dot(value, pair_of((d_low, d_high), g), 1, 1))
    for g in groups:
        masked = jnp.where(alive, scores[g], jnp.float32(-1e30))
        top = jnp.max(masked, axis=0, keepdims=True)
        probs = jnp.exp2((masked - top) * exp2_scale)
        probs = probs * (1.0 / jnp.sum(probs, axis=0, keepdims=True))
        probs_low = probs.astype(jnp.bfloat16)
        delta = jnp.sum(probs_low.astype(jnp.float32) * dprobs[g], axis=0, keepdims=True)
        probs_ref[g] = probs_low
        dscores_ref[g] = (probs * (dprobs[g] - delta)).astype(jnp.bfloat16)
    for g in groups:
        grad_q = (query_scale * dot(keys[g], dscores_ref[g], 0, 0)).astype(jnp.bfloat16)
        for i in range(2):
            spot = (2 * g + i) * HD
            grad_ref[spot : spot + HD, :] = grad_q[:, i * rows : (i + 1) * rows]

    for w_ref, part_ref in zip(w_refs, part_refs):
        block = w_ref[: part_ref.shape[0], :]
        part_ref[...] = dot(block, grad_ref[...], 1, 0).astype(jnp.bfloat16)


def rest_kernel(n_other, grad_ref, *refs):
    for w_ref, part_ref in zip(refs[:n_other], refs[n_other:]):
        block = w_ref[w_ref.shape[0] - part_ref.shape[0] :, :]
        part_ref[...] = dot(block, grad_ref[...], 1, 0).astype(jnp.bfloat16)


def terms_kernel(probs_ref, dscores_ref, q_ref, d_low, d_high, *term_refs):
    held, both = term_refs[0].shape
    width = both // 2
    for g in range(width // HD):
        grad_k = (query_scale * dot(dscores_ref[g], pair_of((q_ref,), g), 1, 0)).astype(jnp.bfloat16)
        grad_v = dot(probs_ref[g], pair_of((d_low, d_high), g), 1, 0).astype(jnp.bfloat16)
        for r, ref in enumerate(term_refs):
            block = slice(r * held, (r + 1) * held)
            ref[:, g * HD : (g + 1) * HD] = grad_k[block]
            ref[:, width + g * HD : width + (g + 1) * HD] = grad_v[block]


def own_kernel(n_head, grad_ref, w_ref, out_ref, w_held, sem):
    feats = out_ref.shape[0]
    start = pl.multiple_of(lax.axis_index("head") * feats, 16)
    copy = pltpu.make_async_copy(w_ref.at[0, pl.ds(start, feats), :], w_held, sem)
    copy.start()
    copy.wait()
    out_ref[...] = dot(w_held[...], grad_ref[...], 1, 0)


def input_sum_kernel(n_other, start, own_ref, *refs):
    arrived = refs[:n_other]
    *_, out_ref, held, sem = refs
    at = slice(start, start + held.shape[0])
    total = own_ref[at, :]
    for ref in arrived:
        total = total + ref[...].astype(jnp.float32)
    held[...] = total.astype(jnp.bfloat16)
    copy = pltpu.make_async_copy(held, out_ref.at[0, at, :], sem)
    copy.start()
    copy.wait()


def term_sum_kernel(*refs):
    *terms, key_ref, value_ref = refs
    total = terms[0][...].astype(jnp.float32)
    for ref in terms[1:]:
        total = total + ref[...].astype(jnp.float32)
    low = total.astype(jnp.bfloat16)
    half = low.shape[1] // 2
    key_ref[0] = low[:, :half]
    value_ref[0] = low[:, half:]


VMEM = pl.BlockSpec(memory_space=pltpu.VMEM)
HBM = pl.BlockSpec(memory_space=pltpu.HBM)


def kernel_call(body, name, out_shape, in_specs, scratch=(), limit=VMEM_LIMIT):
    return pl.pallas_call(
        body,
        out_shape=out_shape,
        in_specs=in_specs,
        out_specs=jax.tree.map(lambda _: VMEM, out_shape),
        scratch_shapes=list(scratch),
        compiler_params=pltpu.CompilerParams(vmem_limit_bytes=limit),
        name=name,
    )


def on_device(queries, grad_out, keys, values, proj_query, section_span, span_prefix):
    n_seq, n_head = lax.axis_size("seq"), lax.axis_size("head")
    n_other = n_head - 1
    direct = n_seq <= MOST_PARTNERS and n_seq & (n_seq - 1) == 0
    low = jnp.bfloat16
    _, held, kv_width = keys.shape
    _, rows, width = queries.shape
    feats = proj_query.shape[1] // n_head

    def shape(*dims, dtype=low):
        return jax.ShapeDtypeStruct(dims, dtype)

    first = feats // 16 * 9 // 16 * 16
    partners = sorted(range(1, n_seq), key=lambda r: -r.bit_length()) if direct else []
    n_copies = 1 + len(partners)
    *joined, grad_low, grad_high = kernel_call(
        functools.partial(join_kernel, n_copies),
        "join",
        [shape(held, 2 * kv_width)] * n_copies + [shape(rows // 2, width)] * 2,
        [HBM] * 3,
        [pltpu.SemaphoreType.DMA((4,))],
    )(*[in_hbm(x) for x in (keys, values, grad_out)])
    if direct:
        blocks = joined[-1:] + [swapped(x, "seq", r) for x, r in zip(joined, partners)]
    else:
        blocks = [lax.all_gather(joined[0], "seq", axis=0, tiled=True)]
    n_blocks, block_rows = len(blocks), blocks[0].shape[0]
    incoming = [shifted(part, "section", -1) for part in (grad_low, grad_high)]

    limit, q, *w_other = kernel_call(
        functools.partial(stage_kernel, n_head),
        "stage",
        [shape(8, HD, dtype=jnp.int32), shape(rows, width)] + [shape(feats, width)] * n_other,
        [HBM] * 4,
        [
            pltpu.SMEM(section_span.shape, jnp.int32),
            pltpu.SMEM(span_prefix.shape, jnp.int32),
            pltpu.SemaphoreType.DMA((1 + n_other,)),
            pltpu.SemaphoreType.DMA((2,)),
        ],
    )(*[in_hbm(x) for x in (section_span, span_prefix, queries, proj_query)])

    prefix = n_blocks * block_rows
    weights = shape(kv_width // HD, prefix, 2 * rows)
    grad_query, probs, dscores, *products = kernel_call(
        functools.partial(attention_kernel, partners, n_other),
        "attention",
        [shape(width, rows), weights, weights] + [shape(first, rows)] * n_other,
        [VMEM] * (4 + n_blocks + n_other),
    )(limit, q, *blocks, *incoming, *w_other)
    rest = kernel_call(
        functools.partial(rest_kernel, n_other),
        "rest",
        [shape(feats - first, rows)] * n_other,
        [VMEM] * (1 + n_other),
    )(grad_query, *w_other)
    arrived = [shifted(p, "head", r + 1) for part in (products, rest) for r, p in enumerate(part)]
    terms = kernel_call(
        terms_kernel, "terms", [shape(block_rows, 2 * kv_width)] * n_blocks, [VMEM] * 5
    )(probs, dscores, q, *incoming)
    if direct:
        sent = sorted(zip(partners, terms[1:]), key=lambda pair: pair[0])
        all_terms = [terms[0]] + [swapped(x, "seq", r) for r, x in sent]
    else:
        all_terms = [lax.psum_scatter(terms[0], "seq", scatter_dimension=0, tiled=True)]

    own = kernel_call(
        functools.partial(own_kernel, n_head),
        "own",
        shape(feats, rows, dtype=jnp.float32),
        [VMEM, HBM],
        [pltpu.VMEM((feats, width), low), pltpu.SemaphoreType.DMA(())],
    )(grad_query, in_hbm(proj_query))
    grad_key, grad_value = kernel_call(
        term_sum_kernel, "term_sum", [shape(1, held, kv_width)] * 2, [VMEM] * len(all_terms)
    )(*all_terms)
    grad_input = []
    for start, part in ((0, arrived[:n_other]), (first, arrived[n_other:])):
        grad_input = [
            pl.pallas_call(
                functools.partial(input_sum_kernel, n_other, start),
                out_shape=shape(1, feats, rows),
                in_specs=[VMEM] * (1 + n_other) + [HBM] * len(grad_input),
                out_specs=HBM,
                scratch_shapes=[pltpu.VMEM(part[0].shape, low), pltpu.SemaphoreType.DMA(())],
                input_output_aliases={1 + n_other: 0} if grad_input else {},
                compiler_params=pltpu.CompilerParams(vmem_limit_bytes=VMEM_LIMIT),
                name="input_sum",
            )(own, *part, *grad_input)
        ]
    grad_input = grad_input[0]
    return (grad_input, grad_key, grad_value)


def solution(mesh):
    in_specs = (
        P("section", "seq", "head"),
        P("section", "seq", "head"),
        P("section", "seq", "head"),
        P("section", "seq", "head"),
        P("section", None, "head"),
        P(),
        P(),
    )
    out_specs = (
        P("section", "head", "seq"),
        P("section", "seq", "head"),
        P("section", "seq", "head"),
    )
    return jax.shard_map(
        on_device, mesh=mesh, in_specs=in_specs, out_specs=out_specs, check_vma=False
    )
```

profile of v0, /device:TPU:0, one launch (start us, length us, event | category | flops | bytes accessed | tf_op | source)
XLA Modules:
  0.0 33.6 jit_solution(12729904266553506166)
XLA Ops:
  0.6 1.0 %join.1 = (bf16[64,768]{1,0:T(8,128)(2,1)S(1)}, bf16[64,768]{1,0:T(8,128)(2,1)S(1)}, bf16[64,768]{1,0:T(8,128)(2,1)S(1)}, bf16[64,768]{1,0:T(8,128)(2,1)S(1)}, b...) custom-call(bf16[1,64,384]{2,1,0:T(8,128)(2,1)} %key_ref.1, bf16[1,64,384]{2,1,0:T(8,128)(2,1)} %value_ref.1, ...), custom_call_target="tpu_custom_call" | custom-call | tf_op jit(solution)/shard_map/join/pallas_call | solution.py:218
  1.7 4.1 %collective-permute-start = (bf16[64,768]{1,0:T(8,128)(2,1)S(1)}, bf16[64,768]{1,0:T(8,128)(2,1)S(1)}, u32[]{:S(2)}, u32[]{:S(2)}) collective-permute-start(bf16[64,768]{1,0:T(8,128)(2,1)S(1)} %get-tuple-element.25), channel_id=1, source_target_pairs={{0,4},{2,6},{4,0},{6,2},{1,5},{3,7},{5,1},{7,3},{8,12},{10,14},{12... | collective-permute-start | bytes 294920 | tf_op jit(solution)/shard_map/ppermute | solution.py:26
  5.8 1.3 %collective-permute-start.1 = (bf16[64,768]{1,0:T(8,128)(2,1)S(1)}, bf16[64,768]{1,0:T(8,128)(2,1)S(1)}, u32[]{:S(2)}, u32[]{:S(2)}) collective-permute-start(bf16[64,768]{1,0:T(8,128)(2,1)S(1)} %get-tuple-element.26), channel_id=1, source_target_pairs={{0,6},{2,4},{4,2},{6,0},{1,7},{3,5},{5,3},{7,1},{8,14},{10,12},{12... | collective-permute-start | bytes 294920 | tf_op jit(solution)/shard_map/ppermute | solution.py:26
  7.1 0.2 collective-permute-start.2
  7.4 0.4 %collective-permute-start.3 = (bf16[64,768]{1,0:T(8,128)(2,1)S(1)}, bf16[64,768]{1,0:T(8,128)(2,1)S(1)}, u32[]{:S(2)}, u32[]{:S(2)}) collective-permute-start(bf16[64,768]{1,0:T(8,128)(2,1)S(1)} %get-tuple-element.28), channel_id=1, source_target_pairs={{8,0},{16,8},{24,16},{0,24},{9,1},{17,9},{25,17},{1,25},{10,2},{18... | collective-permute-start | bytes 294920 | tf_op jit(solution)/shard_map/ppermute | solution.py:22
  7.7 1.2 %collective-permute-start.4 = (bf16[64,768]{1,0:T(8,128)(2,1)S(1)}, bf16[64,768]{1,0:T(8,128)(2,1)S(1)}, u32[]{:S(2)}, u32[]{:S(2)}) collective-permute-start(bf16[64,768]{1,0:T(8,128)(2,1)S(1)} %get-tuple-element.29), channel_id=1, source_target_pairs={{8,0},{16,8},{24,16},{0,24},{9,1},{17,9},{25,17},{1,25},{10,2},{18... | collective-permute-start | bytes 294920 | tf_op jit(solution)/shard_map/ppermute | solution.py:22
  9.0 2.2 %stage.1 = (s32[8,128]{1,0:T(8,128)S(1)}, bf16[128,768]{1,0:T(8,128)(2,1)S(1)}, bf16[2688,768]{1,0:T(8,128)(2,1)S(1)}) custom-call(s32[4]{0:T(128)} %span_ref.1, s32[4]{0:T(128)} %prefix_ref.1, bf16[1,128,768]{2,1,0:T(8,128)(2,1)} %q_ref.1, bf16[1,5376,768]{2,1,0:T(8,128)(2,1)} %w_ref.3), custom_call_target="tpu_custom_call" | custom-call | tf_op jit(solution)/shard_map/stage/pallas_call | solution.py:232
  11.2 2.5 %collective-permute-done.refs_1_ = bf16[64,768]{1,0:T(8,128)(2,1)S(1)} collective-permute-done((bf16[64,768]{1,0:T(8,128)(2,1)S(1)}, bf16[64,768]{1,0:T(8,128)(2,1)S(1)}, u32[]{:S(2)}, u32[]{:S(2)}) %collective-permute-start) | collective-permute-done | bytes 98336 | tf_op jit(solution)/shard_map/ppermute | solution.py:26
  13.7 0.0 collective-permute-done.1.refs_2_
  13.7 0.5 %collective-permute-done.2.refs_3_ = bf16[64,768]{1,0:T(8,128)(2,1)S(1)} collective-permute-done((bf16[64,768]{1,0:T(8,128)(2,1)S(1)}, bf16[64,768]{1,0:T(8,128)(2,1)S(1)}, u32[]{:S(2)}, u32[]{:S(2)}) %collective-permute-start.2) | collective-permute-done | bytes 98336 | tf_op jit(solution)/shard_map/ppermute | solution.py:26
  14.2 0.0 collective-permute-done.3.refs_4_.d_low
  14.2 0.0 collective-permute-done.4.refs_5_.d_high
  14.2 1.6 %attention.1 = (bf16[768,128]{1,0:T(8,128)(2,1)S(1)}, bf16[3,256,256]{2,1,0:T(8,128)(2,1)S(1)}, bf16[3,256,256]{2,1,0:T(8,128)(2,1)S(1)}, bf16[1504,128]{1,0:T(8,128)(2,1)S(1)}) custom-call(s32[8,128]{1,0:T(8,128)S(1)} %get-tuple-element.22.limit_ref, bf16[128,768]{1,0:T(8,128)(2,1)S(1)} %get-tuple-element.23.q_ref, ...), custom_call_target="tpu_custom_call" | custom-call | tf_op jit(solution)/shard_map/attention/pallas_call | solution.py:247
  15.8 1.6 %collective-permute-start.6 = (bf16[1504,128]{1,0:T(8,128)(2,1)S(1)}, bf16[1504,128]{1,0:T(8,128)(2,1)S(1)}, u32[]{:S(2)}, u32[]{:S(2)}) collective-permute-start(bf16[1504,128]{1,0:T(8,128)(2,1)S(1)} %get-tuple-element.32), channel_id=1, source_target_pairs={{1,0},{0,1},{3,2},{2,3},{5,4},{4,5},{7,6},{6,7},{9,8},{8,9},{11,10... | collective-permute-start | bytes 1155080 | tf_op jit(solution)/shard_map/ppermute | solution.py:22
  17.4 0.6 %rest.1 = bf16[1184,128]{1,0:T(8,128)(2,1)S(1)} custom-call(bf16[768,128]{1,0:T(8,128)(2,1)S(1)} %get-tuple-element.31.grad_ref, bf16[2688,768]{1,0:T(8,128)(2,1)S(1)} %get-tuple-element.30.refs_6_.refs_0_), custom_call_target="tpu_custom_call" | custom-call | tf_op jit(solution)/shard_map/rest/pallas_call | solution.py:253
  18.1 0.5 %collective-permute-start.5 = (bf16[1184,128]{1,0:T(8,128)(2,1)S(1)}, bf16[1184,128]{1,0:T(8,128)(2,1)S(1)}, u32[]{:S(2)}, u32[]{:S(2)}) collective-permute-start(bf16[1184,128]{1,0:T(8,128)(2,1)S(1)} %rest.1), channel_id=1, source_target_pairs={{1,0},{0,1},{3,2},{2,3},{5,4},{4,5},{7,6},{6,7},{9,8},{8,9},{11,10... | collective-permute-start | bytes 909320 | tf_op jit(solution)/shard_map/ppermute | solution.py:22
  18.6 0.4 %terms.1 = (bf16[64,768]{1,0:T(8,128)(2,1)S(1)}, bf16[64,768]{1,0:T(8,128)(2,1)S(1)}, bf16[64,768]{1,0:T(8,128)(2,1)S(1)}, bf16[64,768]{1,0:T(8,128)(2,1)S(1)}) custom-call(bf16[3,256,256]{2,1,0:T(8,128)(2,1)S(1)} %get-tuple-element.33.probs_ref, bf16[3,256,256]{2,1,0:T(8,128)(2,1)S(1)} %get-tuple-element.34.dscores_ref, ...), custom_call_target="tpu_custom_call" | custom-call | tf_op jit(solution)/shard_map/terms/pallas_call | solution.py:260
  19.0 1.5 %collective-permute-start.7 = (bf16[64,768]{1,0:T(8,128)(2,1)S(1)}, bf16[64,768]{1,0:T(8,128)(2,1)S(1)}, u32[]{:S(2)}, u32[]{:S(2)}) collective-permute-start(bf16[64,768]{1,0:T(8,128)(2,1)S(1)} %get-tuple-element.36), channel_id=1, source_target_pairs={{0,2},{2,0},{4,6},{6,4},{1,3},{3,1},{5,7},{7,5},{8,10},{10,8},{12,... | collective-permute-start | bytes 294920 | tf_op jit(solution)/shard_map/ppermute | solution.py:26
  20.5 2.4 %collective-permute-start.8 = (bf16[64,768]{1,0:T(8,128)(2,1)S(1)}, bf16[64,768]{1,0:T(8,128)(2,1)S(1)}, u32[]{:S(2)}, u32[]{:S(2)}) collective-permute-start(bf16[64,768]{1,0:T(8,128)(2,1)S(1)} %get-tuple-element.37), channel_id=1, source_target_pairs={{0,4},{2,6},{4,0},{6,2},{1,5},{3,7},{5,1},{7,3},{8,12},{10,14},{12... | collective-permute-start | bytes 294920 | tf_op jit(solution)/shard_map/ppermute | solution.py:26
  22.9 1.0 %collective-permute-start.9 = (bf16[64,768]{1,0:T(8,128)(2,1)S(1)}, bf16[64,768]{1,0:T(8,128)(2,1)S(1)}, u32[]{:S(2)}, u32[]{:S(2)}) collective-permute-start(bf16[64,768]{1,0:T(8,128)(2,1)S(1)} %get-tuple-element.38), channel_id=1, source_target_pairs={{0,6},{2,4},{4,2},{6,0},{1,7},{3,5},{5,3},{7,1},{8,14},{10,12},{12... | collective-permute-start | bytes 294920 | tf_op jit(solution)/shard_map/ppermute | solution.py:26
  23.9 3.4 %own.1.own_ref = f32[2688,128]{1,0:T(8,128)S(1)} custom-call(bf16[768,128]{1,0:T(8,128)(2,1)S(1)} %get-tuple-element.31.grad_ref, bf16[1,5376,768]{2,1,0:T(8,128)(2,1)} %w_ref.3), custom_call_target="tpu_custom_call" | custom-call | tf_op jit(solution)/shard_map/own/pallas_call | solution.py:269
  27.3 0.0 collective-permute-done.7.refs_1_
  27.4 3.9 %collective-permute-done.8.refs_2_ = bf16[64,768]{1,0:T(8,128)(2,1)S(1)} collective-permute-done((bf16[64,768]{1,0:T(8,128)(2,1)S(1)}, bf16[64,768]{1,0:T(8,128)(2,1)S(1)}, u32[]{:S(2)}, u32[]{:S(2)}) %collective-permute-start.8) | collective-permute-done | bytes 98336 | tf_op jit(solution)/shard_map/ppermute | solution.py:26
  31.3 0.0 collective-permute-done.9.refs_3_
  31.3 0.7 %term_sum.1 = (bf16[1,64,384]{2,1,0:T(8,128)(2,1)}, bf16[1,64,384]{2,1,0:T(8,128)(2,1)}) custom-call(bf16[64,768]{1,0:T(8,128)(2,1)S(1)} %get-tuple-element.35.refs_0_, bf16[64,768]{1,0:T(8,128)(2,1)S(1)} %collective-permute-done.7.refs_1_, bf16[64,768]{1,0:T(8,128)(2,1)S(1)} %collective-permute-done.8.refs_2_, ...), custom_call_target="tpu_custom_call" | custom-call | tf_op jit(solution)/shard_map/term_sum/pallas_call | solution.py:276
  31.9 0.0 collective-permute-done.6.refs_0_
  31.9 0.8 %input_sum.2.refs_1_ = bf16[1,2688,128]{2,1,0:T(8,128)(2,1)} custom-call(f32[2688,128]{1,0:T(8,128)S(1)} %own.1.own_ref, bf16[1504,128]{1,0:T(8,128)(2,1)S(1)} %collective-permute-done.6.refs_0_), custom_call_target="tpu_custom_call" | custom-call | tf_op jit(solution)/shard_map/input_sum/pallas_call | solution.py:282
  32.8 0.0 collective-permute-done.5.refs_0_
  32.8 0.8 %input_sum.3 = bf16[1,2688,128]{2,1,0:T(8,128)(2,1)} custom-call(f32[2688,128]{1,0:T(8,128)S(1)} %own.1.own_ref, bf16[1184,128]{1,0:T(8,128)(2,1)S(1)} %collective-permute-done.5.refs_0_, bf16[1,2688,128]{2,1,0:T(8,128)(2,1)} %input_sum.2.refs_1_), custom_call_target="tpu_custom_call", output_to_operand_aliasing={{}: (2, {})} | custom-call | tf_op jit(solution)/shard_map/input_sum/pallas_call | solution.py:282
Async XLA Ops:
  1.7 12.0 %collective-permute-start = (bf16[64,768]{1,0:T(8,128)(2,1)S(1)}, bf16[64,768]{1,0:T(8,128)(2,1)S(1)}, u32[]{:S(2)}, u32[]{:S(2)}) collective-permute-start(bf16[64,768]{1,0:T(8,128)(2,1)S(1)} %get-tuple-element.25), channel_id=1, source_target_pairs={{0,4},{2,6},{4,0},{6,2},{1,5},{3,7},{5,1},{7,3},{8,12},{10,14},{12... | collective-permute-start | bytes 294920 | tf_op jit(solution)/shard_map/ppermute | solution.py:26
  5.8 7.9 %collective-permute-start.1 = (bf16[64,768]{1,0:T(8,128)(2,1)S(1)}, bf16[64,768]{1,0:T(8,128)(2,1)S(1)}, u32[]{:S(2)}, u32[]{:S(2)}) collective-permute-start(bf16[64,768]{1,0:T(8,128)(2,1)S(1)} %get-tuple-element.26), channel_id=1, source_target_pairs={{0,6},{2,4},{4,2},{6,0},{1,7},{3,5},{5,3},{7,1},{8,14},{10,12},{12... | collective-permute-start | bytes 294920 | tf_op jit(solution)/shard_map/ppermute | solution.py:26
  7.1 7.0 %collective-permute-start.2 = (bf16[64,768]{1,0:T(8,128)(2,1)S(1)}, bf16[64,768]{1,0:T(8,128)(2,1)S(1)}, u32[]{:S(2)}, u32[]{:S(2)}) collective-permute-start(bf16[64,768]{1,0:T(8,128)(2,1)S(1)} %get-tuple-element.27), channel_id=1, source_target_pairs={{0,2},{2,0},{4,6},{6,4},{1,3},{3,1},{5,7},{7,5},{8,10},{10,8},{12,... | collective-permute-start | bytes 294920 | tf_op jit(solution)/shard_map/ppermute | solution.py:26
  7.4 6.8 %collective-permute-start.3 = (bf16[64,768]{1,0:T(8,128)(2,1)S(1)}, bf16[64,768]{1,0:T(8,128)(2,1)S(1)}, u32[]{:S(2)}, u32[]{:S(2)}) collective-permute-start(bf16[64,768]{1,0:T(8,128)(2,1)S(1)} %get-tuple-element.28), channel_id=1, source_target_pairs={{8,0},{16,8},{24,16},{0,24},{9,1},{17,9},{25,17},{1,25},{10,2},{18... | collective-permute-start | bytes 294920 | tf_op jit(solution)/shard_map/ppermute | solution.py:22
  7.7 6.5 %collective-permute-start.4 = (bf16[64,768]{1,0:T(8,128)(2,1)S(1)}, bf16[64,768]{1,0:T(8,128)(2,1)S(1)}, u32[]{:S(2)}, u32[]{:S(2)}) collective-permute-start(bf16[64,768]{1,0:T(8,128)(2,1)S(1)} %get-tuple-element.29), channel_id=1, source_target_pairs={{8,0},{16,8},{24,16},{0,24},{9,1},{17,9},{25,17},{1,25},{10,2},{18... | collective-permute-start | bytes 294920 | tf_op jit(solution)/shard_map/ppermute | solution.py:22
  15.8 16.1 %collective-permute-start.6 = (bf16[1504,128]{1,0:T(8,128)(2,1)S(1)}, bf16[1504,128]{1,0:T(8,128)(2,1)S(1)}, u32[]{:S(2)}, u32[]{:S(2)}) collective-permute-start(bf16[1504,128]{1,0:T(8,128)(2,1)S(1)} %get-tuple-element.32), channel_id=1, source_target_pairs={{1,0},{0,1},{3,2},{2,3},{5,4},{4,5},{7,6},{6,7},{9,8},{8,9},{11,10... | collective-permute-start | bytes 1155080 | tf_op jit(solution)/shard_map/ppermute | solution.py:22
  18.1 14.7 %collective-permute-start.5 = (bf16[1184,128]{1,0:T(8,128)(2,1)S(1)}, bf16[1184,128]{1,0:T(8,128)(2,1)S(1)}, u32[]{:S(2)}, u32[]{:S(2)}) collective-permute-start(bf16[1184,128]{1,0:T(8,128)(2,1)S(1)} %rest.1), channel_id=1, source_target_pairs={{1,0},{0,1},{3,2},{2,3},{5,4},{4,5},{7,6},{6,7},{9,8},{8,9},{11,10... | collective-permute-start | bytes 909320 | tf_op jit(solution)/shard_map/ppermute | solution.py:22
  19.0 8.3 %collective-permute-start.7 = (bf16[64,768]{1,0:T(8,128)(2,1)S(1)}, bf16[64,768]{1,0:T(8,128)(2,1)S(1)}, u32[]{:S(2)}, u32[]{:S(2)}) collective-permute-start(bf16[64,768]{1,0:T(8,128)(2,1)S(1)} %get-tuple-element.36), channel_id=1, source_target_pairs={{0,2},{2,0},{4,6},{6,4},{1,3},{3,1},{5,7},{7,5},{8,10},{10,8},{12,... | collective-permute-start | bytes 294920 | tf_op jit(solution)/shard_map/ppermute | solution.py:26
  20.5 10.7 %collective-permute-start.8 = (bf16[64,768]{1,0:T(8,128)(2,1)S(1)}, bf16[64,768]{1,0:T(8,128)(2,1)S(1)}, u32[]{:S(2)}, u32[]{:S(2)}) collective-permute-start(bf16[64,768]{1,0:T(8,128)(2,1)S(1)} %get-tuple-element.37), channel_id=1, source_target_pairs={{0,4},{2,6},{4,0},{6,2},{1,5},{3,7},{5,1},{7,3},{8,12},{10,14},{12... | collective-permute-start | bytes 294920 | tf_op jit(solution)/shard_map/ppermute | solution.py:26
  22.9 8.3 %collective-permute-start.9 = (bf16[64,768]{1,0:T(8,128)(2,1)S(1)}, bf16[64,768]{1,0:T(8,128)(2,1)S(1)}, u32[]{:S(2)}, u32[]{:S(2)}) collective-permute-start(bf16[64,768]{1,0:T(8,128)(2,1)S(1)} %get-tuple-element.38), channel_id=1, source_target_pairs={{0,6},{2,4},{4,2},{6,0},{1,7},{3,5},{5,3},{7,1},{8,14},{10,12},{12... | collective-permute-start | bytes 294920 | tf_op jit(solution)/shard_map/ppermute | solution.py:26
where the time goes:
time: 33.8 us; the launch traced here: 33.6 us
  starting transfers between devices  14.4 us (43%)
  Pallas kernels  11.6 us (34%)
  waiting for transfers between devices  6.92 us (20%)
  between operations  0.71 us (2%)
    ppermute x6, starting transfers between devices, swapped(): lax.ppermute(block, axis, [(i, i ^ distance) for i in range(lax.axis_size...  10.6 us
    ppermute x6, waiting for transfers between devices, swapped(): lax.ppermute(block, axis, [(i, i ^ distance) for i in range(lax.axis_size...  6.91 us
    ppermute x4, starting transfers between devices, shifted(): return lax.ppermute(block, axis, route)  3.79 us
    pallas_call x1, Pallas kernels, on_device(): kernel_call(functools.partial(own_kernel, n_head), 'own', shape(feats, ro...  3.42 us
    pallas_call x1, Pallas kernels, on_device(): kernel_call(functools.partial(stage_kernel, n_head), 'stage', [shape(8, H...  2.21 us
    pallas_call x1, Pallas kernels, on_device(): kernel_call(functools.partial(attention_kernel, partners, n_other), 'atte...  1.62 us
    pallas_call x2, Pallas kernels, on_device(): pl.pallas_call(functools.partial(input_sum_kernel, n_other, start), out_s...  1.61 us
    pallas_call x1, Pallas kernels, on_device(): kernel_call(functools.partial(join_kernel, n_copies), 'join', [shape(held...  1.04 us
  transfers between devices with their start and end apart: 10, of which 3 were waited for; matrix products, arithmetic and copies ran while one was open for 0% of the time, Pallas kernels for 24%

commit v1 on v0

--- a/solution.py
+++ b/solution.py
@@ -213,7 +213,7 @@
         return jax.ShapeDtypeStruct(dims, dtype)
 
     first = feats // 16 * 9 // 16 * 16
-    partners = sorted(range(1, n_seq), key=lambda r: -r.bit_length()) if direct else []
+    partners = list(range(n_seq - 1, 0, -1)) if direct else []
     n_copies = 1 + len(partners)
     *joined, grad_low, grad_high = kernel_call(
         functools.partial(join_kernel, n_copies),

time: 33.8 us -> 34.2 us (1.012)
  waiting for transfers between devices: 6.92 us -> 7.64 us
    ppermute x4, waiting for transfers between devices: 0.01 us -> 2.21 us  [shifted(): return lax.ppermute(block, axis, route)]
    ppermute x6, waiting for transfers between devices: 6.91 us -> 5.43 us  [swapped(): lax.ppermute(block, axis, [(i, i ^ distance) for i in range(lax.axis_size...]
    ppermute x6, starting transfers between devices: 10.6 us -> 10.2 us  [swapped(): lax.ppermute(block, axis, [(i, i ^ distance) for i in range(lax.axis_size...]
  transfers between devices with their start and end apart: 10 -> 10, of which waited for: 3 -> 4; matrix products, arithmetic and copies ran while one was open for 0% -> 0% of each run, Pallas kernels for 24% -> 24%
where the time goes in v1:
time: 34.2 us; the launch traced here: 34 us
  starting transfers between devices  14.1 us (41%)
  Pallas kernels  11.6 us (34%)
  waiting for transfers between devices  7.64 us (22%)
  between operations  0.71 us (2%)
    ppermute x6, starting transfers between devices, swapped(): lax.ppermute(block, axis, [(i, i ^ distance) for i in range(lax.axis_size...  10.2 us
    ppermute x6, waiting for transfers between devices, swapped(): lax.ppermute(block, axis, [(i, i ^ distance) for i in range(lax.axis_size...  5.43 us
    ppermute x4, starting transfers between devices, shifted(): return lax.ppermute(block, axis, route)  3.91 us
    pallas_call x1, Pallas kernels, on_device(): kernel_call(functools.partial(own_kernel, n_head), 'own', shape(feats, ro...  3.41 us
    ppermute x4, waiting for transfers between devices, shifted(): return lax.ppermute(block, axis, route)  2.21 us
    pallas_call x1, Pallas kernels, on_device(): kernel_call(functools.partial(stage_kernel, n_head), 'stage', [shape(8, H...  2.21 us
    pallas_call x1, Pallas kernels, on_device(): kernel_call(functools.partial(attention_kernel, partners, n_other), 'atte...  1.63 us
    pallas_call x2, Pallas kernels, on_device(): pl.pallas_call(functools.partial(input_sum_kernel, n_other, start), out_s...  1.61 us
  transfers between devices with their start and end apart: 10, of which 4 were waited for; matrix products, arithmetic and copies ran while one was open for 0% of the time, Pallas kernels for 24%

profile of v1, /device:TPU:0, one launch (start us, length us, event | category | flops | bytes accessed | tf_op | source)
XLA Modules:
  0.0 34.0 jit_solution(2725762043799991480)
XLA Ops:
  0.6 1.0 %join.1 = (bf16[64,768]{1,0:T(8,128)(2,1)S(1)}, bf16[64,768]{1,0:T(8,128)(2,1)S(1)}, bf16[64,768]{1,0:T(8,128)(2,1)S(1)}, bf16[64,768]{1,0:T(8,128)(2,1)S(1)}, b...) custom-call(bf16[1,64,384]{2,1,0:T(8,128)(2,1)} %key_ref.1, bf16[1,64,384]{2,1,0:T(8,128)(2,1)} %value_ref.1, ...), custom_call_target="tpu_custom_call" | custom-call | tf_op jit(solution)/shard_map/join/pallas_call | solution.py:218
  1.7 5.1 %collective-permute-start = (bf16[64,768]{1,0:T(8,128)(2,1)S(1)}, bf16[64,768]{1,0:T(8,128)(2,1)S(1)}, u32[]{:S(2)}, u32[]{:S(2)}) collective-permute-start(bf16[64,768]{1,0:T(8,128)(2,1)S(1)} %get-tuple-element.25), channel_id=1, source_target_pairs={{0,6},{2,4},{4,2},{6,0},{1,7},{3,5},{5,3},{7,1},{8,14},{10,12},{12... | collective-permute-start | bytes 294920 | tf_op jit(solution)/shard_map/ppermute | solution.py:26
  6.8 0.0 collective-permute-start.1
  6.8 0.6 %collective-permute-start.2 = (bf16[64,768]{1,0:T(8,128)(2,1)S(1)}, bf16[64,768]{1,0:T(8,128)(2,1)S(1)}, u32[]{:S(2)}, u32[]{:S(2)}) collective-permute-start(bf16[64,768]{1,0:T(8,128)(2,1)S(1)} %get-tuple-element.27), channel_id=1, source_target_pairs={{0,2},{2,0},{4,6},{6,4},{1,3},{3,1},{5,7},{7,5},{8,10},{10,8},{12,... | collective-permute-start | bytes 294920 | tf_op jit(solution)/shard_map/ppermute | solution.py:26
  7.4 0.4 %collective-permute-start.3 = (bf16[64,768]{1,0:T(8,128)(2,1)S(1)}, bf16[64,768]{1,0:T(8,128)(2,1)S(1)}, u32[]{:S(2)}, u32[]{:S(2)}) collective-permute-start(bf16[64,768]{1,0:T(8,128)(2,1)S(1)} %get-tuple-element.28), channel_id=1, source_target_pairs={{8,0},{16,8},{24,16},{0,24},{9,1},{17,9},{25,17},{1,25},{10,2},{18... | collective-permute-start | bytes 294920 | tf_op jit(solution)/shard_map/ppermute | solution.py:22
  7.8 1.4 %collective-permute-start.4 = (bf16[64,768]{1,0:T(8,128)(2,1)S(1)}, bf16[64,768]{1,0:T(8,128)(2,1)S(1)}, u32[]{:S(2)}, u32[]{:S(2)}) collective-permute-start(bf16[64,768]{1,0:T(8,128)(2,1)S(1)} %get-tuple-element.29), channel_id=1, source_target_pairs={{8,0},{16,8},{24,16},{0,24},{9,1},{17,9},{25,17},{1,25},{10,2},{18... | collective-permute-start | bytes 294920 | tf_op jit(solution)/shard_map/ppermute | solution.py:22
  9.2 2.2 %stage.1 = (s32[8,128]{1,0:T(8,128)S(1)}, bf16[128,768]{1,0:T(8,128)(2,1)S(1)}, bf16[2688,768]{1,0:T(8,128)(2,1)S(1)}) custom-call(s32[4]{0:T(128)} %span_ref.1, s32[4]{0:T(128)} %prefix_ref.1, bf16[1,128,768]{2,1,0:T(8,128)(2,1)} %q_ref.1, bf16[1,5376,768]{2,1,0:T(8,128)(2,1)} %w_ref.3), custom_call_target="tpu_custom_call" | custom-call | tf_op jit(solution)/shard_map/stage/pallas_call | solution.py:232
  11.4 0.0 collective-permute-done.refs_1_
  11.4 3.6 %collective-permute-done.1.refs_2_ = bf16[64,768]{1,0:T(8,128)(2,1)S(1)} collective-permute-done((bf16[64,768]{1,0:T(8,128)(2,1)S(1)}, bf16[64,768]{1,0:T(8,128)(2,1)S(1)}, u32[]{:S(2)}, u32[]{:S(2)}) %collective-permute-start.1) | collective-permute-done | bytes 98336 | tf_op jit(solution)/shard_map/ppermute | solution.py:26
  15.1 0.0 collective-permute-done.2.refs_3_
  15.1 0.0 collective-permute-done.3.refs_4_.d_low
  15.1 0.0 collective-permute-done.4.refs_5_.d_high
  15.1 1.6 %attention.1 = (bf16[768,128]{1,0:T(8,128)(2,1)S(1)}, bf16[3,256,256]{2,1,0:T(8,128)(2,1)S(1)}, bf16[3,256,256]{2,1,0:T(8,128)(2,1)S(1)}, bf16[1504,128]{1,0:T(8,128)(2,1)S(1)}) custom-call(s32[8,128]{1,0:T(8,128)S(1)} %get-tuple-element.22.limit_ref, bf16[128,768]{1,0:T(8,128)(2,1)S(1)} %get-tuple-element.23.q_ref, ...), custom_call_target="tpu_custom_call" | custom-call | tf_op jit(solution)/shard_map/attention/pallas_call | solution.py:247
  16.7 1.6 %collective-permute-start.6 = (bf16[1504,128]{1,0:T(8,128)(2,1)S(1)}, bf16[1504,128]{1,0:T(8,128)(2,1)S(1)}, u32[]{:S(2)}, u32[]{:S(2)}) collective-permute-start(bf16[1504,128]{1,0:T(8,128)(2,1)S(1)} %get-tuple-element.32), channel_id=1, source_target_pairs={{1,0},{0,1},{3,2},{2,3},{5,4},{4,5},{7,6},{6,7},{9,8},{8,9},{11,10... | collective-permute-start | bytes 1155080 | tf_op jit(solution)/shard_map/ppermute | solution.py:22
  18.3 0.6 %rest.1 = bf16[1184,128]{1,0:T(8,128)(2,1)S(1)} custom-call(bf16[768,128]{1,0:T(8,128)(2,1)S(1)} %get-tuple-element.31.grad_ref, bf16[2688,768]{1,0:T(8,128)(2,1)S(1)} %get-tuple-element.30.refs_6_.refs_0_), custom_call_target="tpu_custom_call" | custom-call | tf_op jit(solution)/shard_map/rest/pallas_call | solution.py:253
  18.9 0.6 %collective-permute-start.5 = (bf16[1184,128]{1,0:T(8,128)(2,1)S(1)}, bf16[1184,128]{1,0:T(8,128)(2,1)S(1)}, u32[]{:S(2)}, u32[]{:S(2)}) collective-permute-start(bf16[1184,128]{1,0:T(8,128)(2,1)S(1)} %rest.1), channel_id=1, source_target_pairs={{1,0},{0,1},{3,2},{2,3},{5,4},{4,5},{7,6},{6,7},{9,8},{8,9},{11,10... | collective-permute-start | bytes 909320 | tf_op jit(solution)/shard_map/ppermute | solution.py:22
  19.5 0.4 %terms.1 = (bf16[64,768]{1,0:T(8,128)(2,1)S(1)}, bf16[64,768]{1,0:T(8,128)(2,1)S(1)}, bf16[64,768]{1,0:T(8,128)(2,1)S(1)}, bf16[64,768]{1,0:T(8,128)(2,1)S(1)}) custom-call(bf16[3,256,256]{2,1,0:T(8,128)(2,1)S(1)} %get-tuple-element.33.probs_ref, bf16[3,256,256]{2,1,0:T(8,128)(2,1)S(1)} %get-tuple-element.34.dscores_ref, ...), custom_call_target="tpu_custom_call" | custom-call | tf_op jit(solution)/shard_map/terms/pallas_call | solution.py:260
  19.9 0.6 %collective-permute-start.7 = (bf16[64,768]{1,0:T(8,128)(2,1)S(1)}, bf16[64,768]{1,0:T(8,128)(2,1)S(1)}, u32[]{:S(2)}, u32[]{:S(2)}) collective-permute-start(bf16[64,768]{1,0:T(8,128)(2,1)S(1)} %get-tuple-element.36), channel_id=1, source_target_pairs={{0,2},{2,0},{4,6},{6,4},{1,3},{3,1},{5,7},{7,5},{8,10},{10,8},{12,... | collective-permute-start | bytes 294920 | tf_op jit(solution)/shard_map/ppermute | solution.py:26
  20.5 2.6 %collective-permute-start.8 = (bf16[64,768]{1,0:T(8,128)(2,1)S(1)}, bf16[64,768]{1,0:T(8,128)(2,1)S(1)}, u32[]{:S(2)}, u32[]{:S(2)}) collective-permute-start(bf16[64,768]{1,0:T(8,128)(2,1)S(1)} %get-tuple-element.37), channel_id=1, source_target_pairs={{0,4},{2,6},{4,0},{6,2},{1,5},{3,7},{5,1},{7,3},{8,12},{10,14},{12... | collective-permute-start | bytes 294920 | tf_op jit(solution)/shard_map/ppermute | solution.py:26
  23.0 1.3 %collective-permute-start.9 = (bf16[64,768]{1,0:T(8,128)(2,1)S(1)}, bf16[64,768]{1,0:T(8,128)(2,1)S(1)}, u32[]{:S(2)}, u32[]{:S(2)}) collective-permute-start(bf16[64,768]{1,0:T(8,128)(2,1)S(1)} %get-tuple-element.38), channel_id=1, source_target_pairs={{0,6},{2,4},{4,2},{6,0},{1,7},{3,5},{5,3},{7,1},{8,14},{10,12},{12... | collective-permute-start | bytes 294920 | tf_op jit(solution)/shard_map/ppermute | solution.py:26
  24.3 3.4 %own.1.own_ref = f32[2688,128]{1,0:T(8,128)S(1)} custom-call(bf16[768,128]{1,0:T(8,128)(2,1)S(1)} %get-tuple-element.31.grad_ref, bf16[1,5376,768]{2,1,0:T(8,128)(2,1)} %w_ref.3), custom_call_target="tpu_custom_call" | custom-call | tf_op jit(solution)/shard_map/own/pallas_call | solution.py:269
  27.7 0.0 collective-permute-done.7.refs_1_
  27.8 0.7 %collective-permute-done.8.refs_2_ = bf16[64,768]{1,0:T(8,128)(2,1)S(1)} collective-permute-done((bf16[64,768]{1,0:T(8,128)(2,1)S(1)}, bf16[64,768]{1,0:T(8,128)(2,1)S(1)}, u32[]{:S(2)}, u32[]{:S(2)}) %collective-permute-start.8) | collective-permute-done | bytes 98336 | tf_op jit(solution)/shard_map/ppermute | solution.py:26
  28.4 1.1 %collective-permute-done.9.refs_3_ = bf16[64,768]{1,0:T(8,128)(2,1)S(1)} collective-permute-done((bf16[64,768]{1,0:T(8,128)(2,1)S(1)}, bf16[64,768]{1,0:T(8,128)(2,1)S(1)}, u32[]{:S(2)}, u32[]{:S(2)}) %collective-permute-start.9) | collective-permute-done | bytes 98336 | tf_op jit(solution)/shard_map/ppermute | solution.py:26
  29.5 0.7 %term_sum.1 = (bf16[1,64,384]{2,1,0:T(8,128)(2,1)}, bf16[1,64,384]{2,1,0:T(8,128)(2,1)}) custom-call(bf16[64,768]{1,0:T(8,128)(2,1)S(1)} %get-tuple-element.35.refs_0_, bf16[64,768]{1,0:T(8,128)(2,1)S(1)} %collective-permute-done.7.refs_1_, bf16[64,768]{1,0:T(8,128)(2,1)S(1)} %collective-permute-done.8.refs_2_, ...), custom_call_target="tpu_custom_call" | custom-call | tf_op jit(solution)/shard_map/term_sum/pallas_call | solution.py:276
  30.2 0.0 collective-permute-done.6.refs_0_
  30.2 0.8 %input_sum.2.refs_1_ = bf16[1,2688,128]{2,1,0:T(8,128)(2,1)} custom-call(f32[2688,128]{1,0:T(8,128)S(1)} %own.1.own_ref, bf16[1504,128]{1,0:T(8,128)(2,1)S(1)} %collective-permute-done.6.refs_0_), custom_call_target="tpu_custom_call" | custom-call | tf_op jit(solution)/shard_map/input_sum/pallas_call | solution.py:282
  31.0 2.2 %collective-permute-done.5.refs_0_ = bf16[1184,128]{1,0:T(8,128)(2,1)S(1)} collective-permute-done((bf16[1184,128]{1,0:T(8,128)(2,1)S(1)}, bf16[1184,128]{1,0:T(8,128)(2,1)S(1)}, u32[]{:S(2)}, u32[]{:S(2)}) %collective-permute-start.5) | collective-permute-done | bytes 303136 | tf_op jit(solution)/shard_map/ppermute | solution.py:22
  33.3 0.8 %input_sum.3 = bf16[1,2688,128]{2,1,0:T(8,128)(2,1)} custom-call(f32[2688,128]{1,0:T(8,128)S(1)} %own.1.own_ref, bf16[1184,128]{1,0:T(8,128)(2,1)S(1)} %collective-permute-done.5.refs_0_, bf16[1,2688,128]{2,1,0:T(8,128)(2,1)} %input_sum.2.refs_1_), custom_call_target="tpu_custom_call", output_to_operand_aliasing={{}: (2, {})} | custom-call | tf_op jit(solution)/shard_map/input_sum/pallas_call | solution.py:282
Async XLA Ops:
  1.7 9.7 %collective-permute-start = (bf16[64,768]{1,0:T(8,128)(2,1)S(1)}, bf16[64,768]{1,0:T(8,128)(2,1)S(1)}, u32[]{:S(2)}, u32[]{:S(2)}) collective-permute-start(bf16[64,768]{1,0:T(8,128)(2,1)S(1)} %get-tuple-element.25), channel_id=1, source_target_pairs={{0,6},{2,4},{4,2},{6,0},{1,7},{3,5},{5,3},{7,1},{8,14},{10,12},{12... | collective-permute-start | bytes 294920 | tf_op jit(solution)/shard_map/ppermute | solution.py:26
  6.8 8.3 %collective-permute-start.1 = (bf16[64,768]{1,0:T(8,128)(2,1)S(1)}, bf16[64,768]{1,0:T(8,128)(2,1)S(1)}, u32[]{:S(2)}, u32[]{:S(2)}) collective-permute-start(bf16[64,768]{1,0:T(8,128)(2,1)S(1)} %get-tuple-element.26), channel_id=1, source_target_pairs={{0,4},{2,6},{4,0},{6,2},{1,5},{3,7},{5,1},{7,3},{8,12},{10,14},{12... | collective-permute-start | bytes 294920 | tf_op jit(solution)/shard_map/ppermute | solution.py:26
  6.8 8.3 %collective-permute-start.2 = (bf16[64,768]{1,0:T(8,128)(2,1)S(1)}, bf16[64,768]{1,0:T(8,128)(2,1)S(1)}, u32[]{:S(2)}, u32[]{:S(2)}) collective-permute-start(bf16[64,768]{1,0:T(8,128)(2,1)S(1)} %get-tuple-element.27), channel_id=1, source_target_pairs={{0,2},{2,0},{4,6},{6,4},{1,3},{3,1},{5,7},{7,5},{8,10},{10,8},{12,... | collective-permute-start | bytes 294920 | tf_op jit(solution)/shard_map/ppermute | solution.py:26
  7.4 7.6 %collective-permute-start.3 = (bf16[64,768]{1,0:T(8,128)(2,1)S(1)}, bf16[64,768]{1,0:T(8,128)(2,1)S(1)}, u32[]{:S(2)}, u32[]{:S(2)}) collective-permute-start(bf16[64,768]{1,0:T(8,128)(2,1)S(1)} %get-tuple-element.28), channel_id=1, source_target_pairs={{8,0},{16,8},{24,16},{0,24},{9,1},{17,9},{25,17},{1,25},{10,2},{18... | collective-permute-start | bytes 294920 | tf_op jit(solution)/shard_map/ppermute | solution.py:22
  7.8 7.3 %collective-permute-start.4 = (bf16[64,768]{1,0:T(8,128)(2,1)S(1)}, bf16[64,768]{1,0:T(8,128)(2,1)S(1)}, u32[]{:S(2)}, u32[]{:S(2)}) collective-permute-start(bf16[64,768]{1,0:T(8,128)(2,1)S(1)} %get-tuple-element.29), channel_id=1, source_target_pairs={{8,0},{16,8},{24,16},{0,24},{9,1},{17,9},{25,17},{1,25},{10,2},{18... | collective-permute-start | bytes 294920 | tf_op jit(solution)/shard_map/ppermute | solution.py:22
  16.7 13.5 %collective-permute-start.6 = (bf16[1504,128]{1,0:T(8,128)(2,1)S(1)}, bf16[1504,128]{1,0:T(8,128)(2,1)S(1)}, u32[]{:S(2)}, u32[]{:S(2)}) collective-permute-start(bf16[1504,128]{1,0:T(8,128)(2,1)S(1)} %get-tuple-element.32), channel_id=1, source_target_pairs={{1,0},{0,1},{3,2},{2,3},{5,4},{4,5},{7,6},{6,7},{9,8},{8,9},{11,10... | collective-permute-start | bytes 1155080 | tf_op jit(solution)/shard_map/ppermute | solution.py:22
  18.9 14.3 %collective-permute-start.5 = (bf16[1184,128]{1,0:T(8,128)(2,1)S(1)}, bf16[1184,128]{1,0:T(8,128)(2,1)S(1)}, u32[]{:S(2)}, u32[]{:S(2)}) collective-permute-start(bf16[1184,128]{1,0:T(8,128)(2,1)S(1)} %rest.1), channel_id=1, source_target_pairs={{1,0},{0,1},{3,2},{2,3},{5,4},{4,5},{7,6},{6,7},{9,8},{8,9},{11,10... | collective-permute-start | bytes 909320 | tf_op jit(solution)/shard_map/ppermute | solution.py:22
  19.9 7.9 %collective-permute-start.7 = (bf16[64,768]{1,0:T(8,128)(2,1)S(1)}, bf16[64,768]{1,0:T(8,128)(2,1)S(1)}, u32[]{:S(2)}, u32[]{:S(2)}) collective-permute-start(bf16[64,768]{1,0:T(8,128)(2,1)S(1)} %get-tuple-element.36), channel_id=1, source_target_pairs={{0,2},{2,0},{4,6},{6,4},{1,3},{3,1},{5,7},{7,5},{8,10},{10,8},{12,... | collective-permute-start | bytes 294920 | tf_op jit(solution)/shard_map/ppermute | solution.py:26
  20.5 8.0 %collective-permute-start.8 = (bf16[64,768]{1,0:T(8,128)(2,1)S(1)}, bf16[64,768]{1,0:T(8,128)(2,1)S(1)}, u32[]{:S(2)}, u32[]{:S(2)}) collective-permute-start(bf16[64,768]{1,0:T(8,128)(2,1)S(1)} %get-tuple-element.37), channel_id=1, source_target_pairs={{0,4},{2,6},{4,0},{6,2},{1,5},{3,7},{5,1},{7,3},{8,12},{10,14},{12... | collective-permute-start | bytes 294920 | tf_op jit(solution)/shard_map/ppermute | solution.py:26
  23.0 6.5 %collective-permute-start.9 = (bf16[64,768]{1,0:T(8,128)(2,1)S(1)}, bf16[64,768]{1,0:T(8,128)(2,1)S(1)}, u32[]{:S(2)}, u32[]{:S(2)}) collective-permute-start(bf16[64,768]{1,0:T(8,128)(2,1)S(1)} %get-tuple-element.38), channel_id=1, source_target_pairs={{0,6},{2,4},{4,2},{6,0},{1,7},{3,5},{5,3},{7,1},{8,14},{10,12},{12... | collective-permute-start | bytes 294920 | tf_op jit(solution)/shard_map/ppermute | solution.py:26

commit v2 on v1

--- a/solution.py
+++ b/solution.py
@@ -213,7 +213,7 @@
         return jax.ShapeDtypeStruct(dims, dtype)
 
     first = feats // 16 * 9 // 16 * 16
-    partners = list(range(n_seq - 1, 0, -1)) if direct else []
+    partners = list(range(1, n_seq)) if direct else []
     n_copies = 1 + len(partners)
     *joined, grad_low, grad_high = kernel_call(
         functools.partial(join_kernel, n_copies),

time: 34.2 us -> 33.2 us (0.971)
  waiting for transfers between devices: 7.64 us -> 6.58 us
    ppermute x4, waiting for transfers between devices: 2.21 us -> 0.32 us  [shifted(): return lax.ppermute(block, axis, route)]
    ppermute x6, waiting for transfers between devices: 5.43 us -> 6.27 us  [swapped(): lax.ppermute(block, axis, [(i, i ^ distance) for i in range(lax.axis_size...]
  transfers between devices with their start and end apart: 10 -> 10, of which waited for: 4 -> 3; matrix products, arithmetic and copies ran while one was open for 0% -> 0% of each run, Pallas kernels for 24% -> 25%
where the time goes in v2:
time: 33.2 us; the launch traced here: 33 us
  starting transfers between devices  14.1 us (42%)
  Pallas kernels  11.6 us (35%)
  waiting for transfers between devices  6.58 us (20%)
  between operations  0.71 us (2%)
    ppermute x6, starting transfers between devices, swapped(): lax.ppermute(block, axis, [(i, i ^ distance) for i in range(lax.axis_size...  10.1 us
    ppermute x6, waiting for transfers between devices, swapped(): lax.ppermute(block, axis, [(i, i ^ distance) for i in range(lax.axis_size...  6.27 us
    ppermute x4, starting transfers between devices, shifted(): return lax.ppermute(block, axis, route)  3.98 us
    pallas_call x1, Pallas kernels, on_device(): kernel_call(functools.partial(own_kernel, n_head), 'own', shape(feats, ro...  3.41 us
    pallas_call x1, Pallas kernels, on_device(): kernel_call(functools.partial(stage_kernel, n_head), 'stage', [shape(8, H...  2.21 us
    pallas_call x1, Pallas kernels, on_device(): kernel_call(functools.partial(attention_kernel, partners, n_other), 'atte...  1.62 us
    pallas_call x2, Pallas kernels, on_device(): pl.pallas_call(functools.partial(input_sum_kernel, n_other, start), out_s...  1.61 us
    pallas_call x1, Pallas kernels, on_device(): kernel_call(functools.partial(join_kernel, n_copies), 'join', [shape(held...  1.04 us
  transfers between devices with their start and end apart: 10, of which 3 were waited for; matrix products, arithmetic and copies ran while one was open for 0% of the time, Pallas kernels for 25%

profile of v2, /device:TPU:0, one launch (start us, length us, event | category | flops | bytes accessed | tf_op | source)
XLA Modules:
  0.0 33.0 jit_solution(16359883882695221456)
XLA Ops:
  0.6 1.0 %join.1 = (bf16[64,768]{1,0:T(8,128)(2,1)S(1)}, bf16[64,768]{1,0:T(8,128)(2,1)S(1)}, bf16[64,768]{1,0:T(8,128)(2,1)S(1)}, bf16[64,768]{1,0:T(8,128)(2,1)S(1)}, b...) custom-call(bf16[1,64,384]{2,1,0:T(8,128)(2,1)} %key_ref.1, bf16[1,64,384]{2,1,0:T(8,128)(2,1)} %value_ref.1, ...), custom_call_target="tpu_custom_call" | custom-call | tf_op jit(solution)/shard_map/join/pallas_call | solution.py:218
  1.7 3.1 %collective-permute-start = (bf16[64,768]{1,0:T(8,128)(2,1)S(1)}, bf16[64,768]{1,0:T(8,128)(2,1)S(1)}, u32[]{:S(2)}, u32[]{:S(2)}) collective-permute-start(bf16[64,768]{1,0:T(8,128)(2,1)S(1)} %get-tuple-element.25), channel_id=1, source_target_pairs={{0,2},{2,0},{4,6},{6,4},{1,3},{3,1},{5,7},{7,5},{8,10},{10,8},{12,... | collective-permute-start | bytes 294920 | tf_op jit(solution)/shard_map/ppermute | solution.py:26
  4.8 2.6 %collective-permute-start.1 = (bf16[64,768]{1,0:T(8,128)(2,1)S(1)}, bf16[64,768]{1,0:T(8,128)(2,1)S(1)}, u32[]{:S(2)}, u32[]{:S(2)}) collective-permute-start(bf16[64,768]{1,0:T(8,128)(2,1)S(1)} %get-tuple-element.26), channel_id=1, source_target_pairs={{0,4},{2,6},{4,0},{6,2},{1,5},{3,7},{5,1},{7,3},{8,12},{10,14},{12... | collective-permute-start | bytes 294920 | tf_op jit(solution)/shard_map/ppermute | solution.py:26
  7.4 0.0 collective-permute-start.2
  7.4 0.4 %collective-permute-start.3 = (bf16[64,768]{1,0:T(8,128)(2,1)S(1)}, bf16[64,768]{1,0:T(8,128)(2,1)S(1)}, u32[]{:S(2)}, u32[]{:S(2)}) collective-permute-start(bf16[64,768]{1,0:T(8,128)(2,1)S(1)} %get-tuple-element.28), channel_id=1, source_target_pairs={{8,0},{16,8},{24,16},{0,24},{9,1},{17,9},{25,17},{1,25},{10,2},{18... | collective-permute-start | bytes 294920 | tf_op jit(solution)/shard_map/ppermute | solution.py:22
  7.7 1.5 %collective-permute-start.4 = (bf16[64,768]{1,0:T(8,128)(2,1)S(1)}, bf16[64,768]{1,0:T(8,128)(2,1)S(1)}, u32[]{:S(2)}, u32[]{:S(2)}) collective-permute-start(bf16[64,768]{1,0:T(8,128)(2,1)S(1)} %get-tuple-element.29), channel_id=1, source_target_pairs={{8,0},{16,8},{24,16},{0,24},{9,1},{17,9},{25,17},{1,25},{10,2},{18... | collective-permute-start | bytes 294920 | tf_op jit(solution)/shard_map/ppermute | solution.py:22
  9.2 2.2 %stage.1 = (s32[8,128]{1,0:T(8,128)S(1)}, bf16[128,768]{1,0:T(8,128)(2,1)S(1)}, bf16[2688,768]{1,0:T(8,128)(2,1)S(1)}) custom-call(s32[4]{0:T(128)} %span_ref.1, s32[4]{0:T(128)} %prefix_ref.1, bf16[1,128,768]{2,1,0:T(8,128)(2,1)} %q_ref.1, bf16[1,5376,768]{2,1,0:T(8,128)(2,1)} %w_ref.3), custom_call_target="tpu_custom_call" | custom-call | tf_op jit(solution)/shard_map/stage/pallas_call | solution.py:232
  11.4 0.0 collective-permute-done.refs_1_
  11.4 3.8 %collective-permute-done.1.refs_2_ = bf16[64,768]{1,0:T(8,128)(2,1)S(1)} collective-permute-done((bf16[64,768]{1,0:T(8,128)(2,1)S(1)}, bf16[64,768]{1,0:T(8,128)(2,1)S(1)}, u32[]{:S(2)}, u32[]{:S(2)}) %collective-permute-start.1) | collective-permute-done | bytes 98336 | tf_op jit(solution)/shard_map/ppermute | solution.py:26
  15.2 0.0 collective-permute-done.2.refs_3_
  15.2 0.0 collective-permute-done.3.refs_4_.d_low
  15.2 0.0 collective-permute-done.4.refs_5_.d_high
  15.2 1.6 %attention.1 = (bf16[768,128]{1,0:T(8,128)(2,1)S(1)}, bf16[3,256,256]{2,1,0:T(8,128)(2,1)S(1)}, bf16[3,256,256]{2,1,0:T(8,128)(2,1)S(1)}, bf16[1504,128]{1,0:T(8,128)(2,1)S(1)}) custom-call(s32[8,128]{1,0:T(8,128)S(1)} %get-tuple-element.22.limit_ref, bf16[128,768]{1,0:T(8,128)(2,1)S(1)} %get-tuple-element.23.q_ref, ...), custom_call_target="tpu_custom_call" | custom-call | tf_op jit(solution)/shard_map/attention/pallas_call | solution.py:247
  16.8 1.6 %collective-permute-start.6 = (bf16[1504,128]{1,0:T(8,128)(2,1)S(1)}, bf16[1504,128]{1,0:T(8,128)(2,1)S(1)}, u32[]{:S(2)}, u32[]{:S(2)}) collective-permute-start(bf16[1504,128]{1,0:T(8,128)(2,1)S(1)} %get-tuple-element.32), channel_id=1, source_target_pairs={{1,0},{0,1},{3,2},{2,3},{5,4},{4,5},{7,6},{6,7},{9,8},{8,9},{11,10... | collective-permute-start | bytes 1155080 | tf_op jit(solution)/shard_map/ppermute | solution.py:22
  18.4 0.6 %rest.1 = bf16[1184,128]{1,0:T(8,128)(2,1)S(1)} custom-call(bf16[768,128]{1,0:T(8,128)(2,1)S(1)} %get-tuple-element.31.grad_ref, bf16[2688,768]{1,0:T(8,128)(2,1)S(1)} %get-tuple-element.30.refs_6_.refs_0_), custom_call_target="tpu_custom_call" | custom-call | tf_op jit(solution)/shard_map/rest/pallas_call | solution.py:253
  19.1 0.6 %collective-permute-start.5 = (bf16[1184,128]{1,0:T(8,128)(2,1)S(1)}, bf16[1184,128]{1,0:T(8,128)(2,1)S(1)}, u32[]{:S(2)}, u32[]{:S(2)}) collective-permute-start(bf16[1184,128]{1,0:T(8,128)(2,1)S(1)} %rest.1), channel_id=1, source_target_pairs={{1,0},{0,1},{3,2},{2,3},{5,4},{4,5},{7,6},{6,7},{9,8},{8,9},{11,10... | collective-permute-start | bytes 909320 | tf_op jit(solution)/shard_map/ppermute | solution.py:22
  19.6 0.4 %terms.1 = (bf16[64,768]{1,0:T(8,128)(2,1)S(1)}, bf16[64,768]{1,0:T(8,128)(2,1)S(1)}, bf16[64,768]{1,0:T(8,128)(2,1)S(1)}, bf16[64,768]{1,0:T(8,128)(2,1)S(1)}) custom-call(bf16[3,256,256]{2,1,0:T(8,128)(2,1)S(1)} %get-tuple-element.33.probs_ref, bf16[3,256,256]{2,1,0:T(8,128)(2,1)S(1)} %get-tuple-element.34.dscores_ref, ...), custom_call_target="tpu_custom_call" | custom-call | tf_op jit(solution)/shard_map/terms/pallas_call | solution.py:260
  20.0 1.7 %collective-permute-start.7 = (bf16[64,768]{1,0:T(8,128)(2,1)S(1)}, bf16[64,768]{1,0:T(8,128)(2,1)S(1)}, u32[]{:S(2)}, u32[]{:S(2)}) collective-permute-start(bf16[64,768]{1,0:T(8,128)(2,1)S(1)} %get-tuple-element.36), channel_id=1, source_target_pairs={{0,2},{2,0},{4,6},{6,4},{1,3},{3,1},{5,7},{7,5},{8,10},{10,8},{12,... | collective-permute-start | bytes 294920 | tf_op jit(solution)/shard_map/ppermute | solution.py:26
  21.7 1.4 %collective-permute-start.8 = (bf16[64,768]{1,0:T(8,128)(2,1)S(1)}, bf16[64,768]{1,0:T(8,128)(2,1)S(1)}, u32[]{:S(2)}, u32[]{:S(2)}) collective-permute-start(bf16[64,768]{1,0:T(8,128)(2,1)S(1)} %get-tuple-element.37), channel_id=1, source_target_pairs={{0,4},{2,6},{4,0},{6,2},{1,5},{3,7},{5,1},{7,3},{8,12},{10,14},{12... | collective-permute-start | bytes 294920 | tf_op jit(solution)/shard_map/ppermute | solution.py:26
  23.1 1.3 %collective-permute-start.9 = (bf16[64,768]{1,0:T(8,128)(2,1)S(1)}, bf16[64,768]{1,0:T(8,128)(2,1)S(1)}, u32[]{:S(2)}, u32[]{:S(2)}) collective-permute-start(bf16[64,768]{1,0:T(8,128)(2,1)S(1)} %get-tuple-element.38), channel_id=1, source_target_pairs={{0,6},{2,4},{4,2},{6,0},{1,7},{3,5},{5,3},{7,1},{8,14},{10,12},{12... | collective-permute-start | bytes 294920 | tf_op jit(solution)/shard_map/ppermute | solution.py:26
  24.5 3.4 %own.1.own_ref = f32[2688,128]{1,0:T(8,128)S(1)} custom-call(bf16[768,128]{1,0:T(8,128)(2,1)S(1)} %get-tuple-element.31.grad_ref, bf16[1,5376,768]{2,1,0:T(8,128)(2,1)} %w_ref.3), custom_call_target="tpu_custom_call" | custom-call | tf_op jit(solution)/shard_map/own/pallas_call | solution.py:269
  27.9 0.0 collective-permute-done.7.refs_1_
  27.9 2.5 %collective-permute-done.8.refs_2_ = bf16[64,768]{1,0:T(8,128)(2,1)S(1)} collective-permute-done((bf16[64,768]{1,0:T(8,128)(2,1)S(1)}, bf16[64,768]{1,0:T(8,128)(2,1)S(1)}, u32[]{:S(2)}, u32[]{:S(2)}) %collective-permute-start.8) | collective-permute-done | bytes 98336 | tf_op jit(solution)/shard_map/ppermute | solution.py:26
  30.4 0.0 collective-permute-done.9.refs_3_
  30.4 0.7 %term_sum.1 = (bf16[1,64,384]{2,1,0:T(8,128)(2,1)}, bf16[1,64,384]{2,1,0:T(8,128)(2,1)}) custom-call(bf16[64,768]{1,0:T(8,128)(2,1)S(1)} %get-tuple-element.35.refs_0_, bf16[64,768]{1,0:T(8,128)(2,1)S(1)} %collective-permute-done.7.refs_1_, bf16[64,768]{1,0:T(8,128)(2,1)S(1)} %collective-permute-done.8.refs_2_, ...), custom_call_target="tpu_custom_call" | custom-call | tf_op jit(solution)/shard_map/term_sum/pallas_call | solution.py:276
  31.0 0.0 collective-permute-done.6.refs_0_
  31.0 0.8 %input_sum.2.refs_1_ = bf16[1,2688,128]{2,1,0:T(8,128)(2,1)} custom-call(f32[2688,128]{1,0:T(8,128)S(1)} %own.1.own_ref, bf16[1504,128]{1,0:T(8,128)(2,1)S(1)} %collective-permute-done.6.refs_0_), custom_call_target="tpu_custom_call" | custom-call | tf_op jit(solution)/shard_map/input_sum/pallas_call | solution.py:282
  31.9 0.3 collective-permute-done.5.refs_0_
  32.2 0.8 %input_sum.3 = bf16[1,2688,128]{2,1,0:T(8,128)(2,1)} custom-call(f32[2688,128]{1,0:T(8,128)S(1)} %own.1.own_ref, bf16[1184,128]{1,0:T(8,128)(2,1)S(1)} %collective-permute-done.5.refs_0_, bf16[1,2688,128]{2,1,0:T(8,128)(2,1)} %input_sum.2.refs_1_), custom_call_target="tpu_custom_call", output_to_operand_aliasing={{}: (2, {})} | custom-call | tf_op jit(solution)/shard_map/input_sum/pallas_call | solution.py:282
Async XLA Ops:
  1.7 9.7 %collective-permute-start = (bf16[64,768]{1,0:T(8,128)(2,1)S(1)}, bf16[64,768]{1,0:T(8,128)(2,1)S(1)}, u32[]{:S(2)}, u32[]{:S(2)}) collective-permute-start(bf16[64,768]{1,0:T(8,128)(2,1)S(1)} %get-tuple-element.25), channel_id=1, source_target_pairs={{0,2},{2,0},{4,6},{6,4},{1,3},{3,1},{5,7},{7,5},{8,10},{10,8},{12,... | collective-permute-start | bytes 294920 | tf_op jit(solution)/shard_map/ppermute | solution.py:26
  4.8 10.4 %collective-permute-start.1 = (bf16[64,768]{1,0:T(8,128)(2,1)S(1)}, bf16[64,768]{1,0:T(8,128)(2,1)S(1)}, u32[]{:S(2)}, u32[]{:S(2)}) collective-permute-start(bf16[64,768]{1,0:T(8,128)(2,1)S(1)} %get-tuple-element.26), channel_id=1, source_target_pairs={{0,4},{2,6},{4,0},{6,2},{1,5},{3,7},{5,1},{7,3},{8,12},{10,14},{12... | collective-permute-start | bytes 294920 | tf_op jit(solution)/shard_map/ppermute | solution.py:26
  7.4 7.8 %collective-permute-start.2 = (bf16[64,768]{1,0:T(8,128)(2,1)S(1)}, bf16[64,768]{1,0:T(8,128)(2,1)S(1)}, u32[]{:S(2)}, u32[]{:S(2)}) collective-permute-start(bf16[64,768]{1,0:T(8,128)(2,1)S(1)} %get-tuple-element.27), channel_id=1, source_target_pairs={{0,6},{2,4},{4,2},{6,0},{1,7},{3,5},{5,3},{7,1},{8,14},{10,12},{12... | collective-permute-start | bytes 294920 | tf_op jit(solution)/shard_map/ppermute | solution.py:26
  7.4 7.8 %collective-permute-start.3 = (bf16[64,768]{1,0:T(8,128)(2,1)S(1)}, bf16[64,768]{1,0:T(8,128)(2,1)S(1)}, u32[]{:S(2)}, u32[]{:S(2)}) collective-permute-start(bf16[64,768]{1,0:T(8,128)(2,1)S(1)} %get-tuple-element.28), channel_id=1, source_target_pairs={{8,0},{16,8},{24,16},{0,24},{9,1},{17,9},{25,17},{1,25},{10,2},{18... | collective-permute-start | bytes 294920 | tf_op jit(solution)/shard_map/ppermute | solution.py:22
  7.7 7.5 %collective-permute-start.4 = (bf16[64,768]{1,0:T(8,128)(2,1)S(1)}, bf16[64,768]{1,0:T(8,128)(2,1)S(1)}, u32[]{:S(2)}, u32[]{:S(2)}) collective-permute-start(bf16[64,768]{1,0:T(8,128)(2,1)S(1)} %get-tuple-element.29), channel_id=1, source_target_pairs={{8,0},{16,8},{24,16},{0,24},{9,1},{17,9},{25,17},{1,25},{10,2},{18... | collective-permute-start | bytes 294920 | tf_op jit(solution)/shard_map/ppermute | solution.py:22
  16.8 14.2 %collective-permute-start.6 = (bf16[1504,128]{1,0:T(8,128)(2,1)S(1)}, bf16[1504,128]{1,0:T(8,128)(2,1)S(1)}, u32[]{:S(2)}, u32[]{:S(2)}) collective-permute-start(bf16[1504,128]{1,0:T(8,128)(2,1)S(1)} %get-tuple-element.32), channel_id=1, source_target_pairs={{1,0},{0,1},{3,2},{2,3},{5,4},{4,5},{7,6},{6,7},{9,8},{8,9},{11,10... | collective-permute-start | bytes 1155080 | tf_op jit(solution)/shard_map/ppermute | solution.py:22
  19.1 13.1 %collective-permute-start.5 = (bf16[1184,128]{1,0:T(8,128)(2,1)S(1)}, bf16[1184,128]{1,0:T(8,128)(2,1)S(1)}, u32[]{:S(2)}, u32[]{:S(2)}) collective-permute-start(bf16[1184,128]{1,0:T(8,128)(2,1)S(1)} %rest.1), channel_id=1, source_target_pairs={{1,0},{0,1},{3,2},{2,3},{5,4},{4,5},{7,6},{6,7},{9,8},{8,9},{11,10... | collective-permute-start | bytes 909320 | tf_op jit(solution)/shard_map/ppermute | solution.py:22
  20.0 7.9 %collective-permute-start.7 = (bf16[64,768]{1,0:T(8,128)(2,1)S(1)}, bf16[64,768]{1,0:T(8,128)(2,1)S(1)}, u32[]{:S(2)}, u32[]{:S(2)}) collective-permute-start(bf16[64,768]{1,0:T(8,128)(2,1)S(1)} %get-tuple-element.36), channel_id=1, source_target_pairs={{0,2},{2,0},{4,6},{6,4},{1,3},{3,1},{5,7},{7,5},{8,10},{10,8},{12,... | collective-permute-start | bytes 294920 | tf_op jit(solution)/shard_map/ppermute | solution.py:26
  21.7 8.7 %collective-permute-start.8 = (bf16[64,768]{1,0:T(8,128)(2,1)S(1)}, bf16[64,768]{1,0:T(8,128)(2,1)S(1)}, u32[]{:S(2)}, u32[]{:S(2)}) collective-permute-start(bf16[64,768]{1,0:T(8,128)(2,1)S(1)} %get-tuple-element.37), channel_id=1, source_target_pairs={{0,4},{2,6},{4,0},{6,2},{1,5},{3,7},{5,1},{7,3},{8,12},{10,14},{12... | collective-permute-start | bytes 294920 | tf_op jit(solution)/shard_map/ppermute | solution.py:26
  23.1 7.3 %collective-permute-start.9 = (bf16[64,768]{1,0:T(8,128)(2,1)S(1)}, bf16[64,768]{1,0:T(8,128)(2,1)S(1)}, u32[]{:S(2)}, u32[]{:S(2)}) collective-permute-start(bf16[64,768]{1,0:T(8,128)(2,1)S(1)} %get-tuple-element.38), channel_id=1, source_target_pairs={{0,6},{2,4},{4,2},{6,0},{1,7},{3,5},{5,3},{7,1},{8,14},{10,12},{12... | collective-permute-start | bytes 294920 | tf_op jit(solution)/shard_map/ppermute | solution.py:26

commit v3 on v2

--- a/solution.py
+++ b/solution.py
@@ -212,7 +212,7 @@
     def shape(*dims, dtype=low):
         return jax.ShapeDtypeStruct(dims, dtype)
 
-    first = feats // 16 * 9 // 16 * 16
+    first = feats // 16 * 17 // 32 * 16
     partners = list(range(1, n_seq)) if direct else []
     n_copies = 1 + len(partners)
     *joined, grad_low, grad_high = kernel_call(
@@ -261,7 +261,7 @@
         terms_kernel, "terms", [shape(block_rows, 2 * kv_width)] * n_blocks, [VMEM] * 5
     )(probs, dscores, q, *incoming)
     if direct:
-        sent = sorted(zip(partners, terms[1:]), key=lambda pair: pair[0])
+        sent = sorted(zip(partners, terms[1:]), key=lambda pair: -pair[0])
         all_terms = [terms[0]] + [swapped(x, "seq", r) for r, x in sent]
     else:
         all_terms = [lax.psum_scatter(terms[0], "seq", scatter_dimension=0, tiled=True)]

time: 33.2 us -> 33.1 us (level)
  no operation moved by 1% of the time
where the time goes in v3:
time: 33.1 us; the launch traced here: 32.9 us
  starting transfers between devices  14.1 us (43%)
  Pallas kernels  11.6 us (35%)
  waiting for transfers between devices  6.57 us (20%)
  between operations  0.71 us (2%)
    ppermute x6, starting transfers between devices, swapped(): lax.ppermute(block, axis, [(i, i ^ distance) for i in range(lax.axis_size...  10.1 us
    ppermute x6, waiting for transfers between devices, swapped(): lax.ppermute(block, axis, [(i, i ^ distance) for i in range(lax.axis_size...  6.17 us
    ppermute x4, starting transfers between devices, shifted(): return lax.ppermute(block, axis, route)  3.98 us
    pallas_call x1, Pallas kernels, on_device(): kernel_call(functools.partial(own_kernel, n_head), 'own', shape(feats, ro...  3.42 us
    pallas_call x1, Pallas kernels, on_device(): kernel_call(functools.partial(stage_kernel, n_head), 'stage', [shape(8, H...  2.21 us
    pallas_call x1, Pallas kernels, on_device(): kernel_call(functools.partial(attention_kernel, partners, n_other), 'atte...  1.6 us
    pallas_call x2, Pallas kernels, on_device(): pl.pallas_call(functools.partial(input_sum_kernel, n_other, start), out_s...  1.59 us
    pallas_call x1, Pallas kernels, on_device(): kernel_call(functools.partial(join_kernel, n_copies), 'join', [shape(held...  1.04 us
  transfers between devices with their start and end apart: 10, of which 3 were waited for; matrix products, arithmetic and copies ran while one was open for 0% of the time, Pallas kernels for 25%

profile of v3, /device:TPU:0, one launch (start us, length us, event | category | flops | bytes accessed | tf_op | source)
XLA Modules:
  0.0 32.9 jit_solution(4705054823461307712)
XLA Ops:
  0.6 1.0 %join.1 = (bf16[64,768]{1,0:T(8,128)(2,1)S(1)}, bf16[64,768]{1,0:T(8,128)(2,1)S(1)}, bf16[64,768]{1,0:T(8,128)(2,1)S(1)}, bf16[64,768]{1,0:T(8,128)(2,1)S(1)}, b...) custom-call(bf16[1,64,384]{2,1,0:T(8,128)(2,1)} %key_ref.1, bf16[1,64,384]{2,1,0:T(8,128)(2,1)} %value_ref.1, ...), custom_call_target="tpu_custom_call" | custom-call | tf_op jit(solution)/shard_map/join/pallas_call | solution.py:218
  1.7 3.1 %collective-permute-start = (bf16[64,768]{1,0:T(8,128)(2,1)S(1)}, bf16[64,768]{1,0:T(8,128)(2,1)S(1)}, u32[]{:S(2)}, u32[]{:S(2)}) collective-permute-start(bf16[64,768]{1,0:T(8,128)(2,1)S(1)} %get-tuple-element.25), channel_id=1, source_target_pairs={{0,2},{2,0},{4,6},{6,4},{1,3},{3,1},{5,7},{7,5},{8,10},{10,8},{12,... | collective-permute-start | bytes 294920 | tf_op jit(solution)/shard_map/ppermute | solution.py:26
  4.8 2.6 %collective-permute-start.1 = (bf16[64,768]{1,0:T(8,128)(2,1)S(1)}, bf16[64,768]{1,0:T(8,128)(2,1)S(1)}, u32[]{:S(2)}, u32[]{:S(2)}) collective-permute-start(bf16[64,768]{1,0:T(8,128)(2,1)S(1)} %get-tuple-element.26), channel_id=1, source_target_pairs={{0,4},{2,6},{4,0},{6,2},{1,5},{3,7},{5,1},{7,3},{8,12},{10,14},{12... | collective-permute-start | bytes 294920 | tf_op jit(solution)/shard_map/ppermute | solution.py:26
  7.4 0.0 collective-permute-start.2
  7.4 0.4 %collective-permute-start.3 = (bf16[64,768]{1,0:T(8,128)(2,1)S(1)}, bf16[64,768]{1,0:T(8,128)(2,1)S(1)}, u32[]{:S(2)}, u32[]{:S(2)}) collective-permute-start(bf16[64,768]{1,0:T(8,128)(2,1)S(1)} %get-tuple-element.28), channel_id=1, source_target_pairs={{8,0},{16,8},{24,16},{0,24},{9,1},{17,9},{25,17},{1,25},{10,2},{18... | collective-permute-start | bytes 294920 | tf_op jit(solution)/shard_map/ppermute | solution.py:22
  7.7 1.5 %collective-permute-start.4 = (bf16[64,768]{1,0:T(8,128)(2,1)S(1)}, bf16[64,768]{1,0:T(8,128)(2,1)S(1)}, u32[]{:S(2)}, u32[]{:S(2)}) collective-permute-start(bf16[64,768]{1,0:T(8,128)(2,1)S(1)} %get-tuple-element.29), channel_id=1, source_target_pairs={{8,0},{16,8},{24,16},{0,24},{9,1},{17,9},{25,17},{1,25},{10,2},{18... | collective-permute-start | bytes 294920 | tf_op jit(solution)/shard_map/ppermute | solution.py:22
  9.2 2.2 %stage.1 = (s32[8,128]{1,0:T(8,128)S(1)}, bf16[128,768]{1,0:T(8,128)(2,1)S(1)}, bf16[2688,768]{1,0:T(8,128)(2,1)S(1)}) custom-call(s32[4]{0:T(128)} %span_ref.1, s32[4]{0:T(128)} %prefix_ref.1, bf16[1,128,768]{2,1,0:T(8,128)(2,1)} %q_ref.1, bf16[1,5376,768]{2,1,0:T(8,128)(2,1)} %w_ref.3), custom_call_target="tpu_custom_call" | custom-call | tf_op jit(solution)/shard_map/stage/pallas_call | solution.py:232
  11.4 0.0 collective-permute-done.refs_1_
  11.4 3.8 %collective-permute-done.1.refs_2_ = bf16[64,768]{1,0:T(8,128)(2,1)S(1)} collective-permute-done((bf16[64,768]{1,0:T(8,128)(2,1)S(1)}, bf16[64,768]{1,0:T(8,128)(2,1)S(1)}, u32[]{:S(2)}, u32[]{:S(2)}) %collective-permute-start.1) | collective-permute-done | bytes 98336 | tf_op jit(solution)/shard_map/ppermute | solution.py:26
  15.2 0.0 collective-permute-done.2.refs_3_
  15.2 0.0 collective-permute-done.3.refs_4_.d_low
  15.2 0.0 collective-permute-done.4.refs_5_.d_high
  15.2 1.6 %attention.1 = (bf16[768,128]{1,0:T(8,128)(2,1)S(1)}, bf16[3,256,256]{2,1,0:T(8,128)(2,1)S(1)}, bf16[3,256,256]{2,1,0:T(8,128)(2,1)S(1)}, bf16[1424,128]{1,0:T(8,128)(2,1)S(1)}) custom-call(s32[8,128]{1,0:T(8,128)S(1)} %get-tuple-element.22.limit_ref, bf16[128,768]{1,0:T(8,128)(2,1)S(1)} %get-tuple-element.23.q_ref, ...), custom_call_target="tpu_custom_call" | custom-call | tf_op jit(solution)/shard_map/attention/pallas_call | solution.py:247
  16.8 1.6 %collective-permute-start.6 = (bf16[1424,128]{1,0:T(8,128)(2,1)S(1)}, bf16[1424,128]{1,0:T(8,128)(2,1)S(1)}, u32[]{:S(2)}, u32[]{:S(2)}) collective-permute-start(bf16[1424,128]{1,0:T(8,128)(2,1)S(1)} %get-tuple-element.32), channel_id=1, source_target_pairs={{1,0},{0,1},{3,2},{2,3},{5,4},{4,5},{7,6},{6,7},{9,8},{8,9},{11,10... | collective-permute-start | bytes 1093640 | tf_op jit(solution)/shard_map/ppermute | solution.py:22
  18.4 0.7 %rest.1 = bf16[1264,128]{1,0:T(8,128)(2,1)S(1)} custom-call(bf16[768,128]{1,0:T(8,128)(2,1)S(1)} %get-tuple-element.31.grad_ref, bf16[2688,768]{1,0:T(8,128)(2,1)S(1)} %get-tuple-element.30.refs_6_.refs_0_), custom_call_target="tpu_custom_call" | custom-call | tf_op jit(solution)/shard_map/rest/pallas_call | solution.py:253
  19.1 0.6 %collective-permute-start.5 = (bf16[1264,128]{1,0:T(8,128)(2,1)S(1)}, bf16[1264,128]{1,0:T(8,128)(2,1)S(1)}, u32[]{:S(2)}, u32[]{:S(2)}) collective-permute-start(bf16[1264,128]{1,0:T(8,128)(2,1)S(1)} %rest.1), channel_id=1, source_target_pairs={{1,0},{0,1},{3,2},{2,3},{5,4},{4,5},{7,6},{6,7},{9,8},{8,9},{11,10... | collective-permute-start | bytes 970760 | tf_op jit(solution)/shard_map/ppermute | solution.py:22
  19.6 0.4 %terms.1 = (bf16[64,768]{1,0:T(8,128)(2,1)S(1)}, bf16[64,768]{1,0:T(8,128)(2,1)S(1)}, bf16[64,768]{1,0:T(8,128)(2,1)S(1)}, bf16[64,768]{1,0:T(8,128)(2,1)S(1)}) custom-call(bf16[3,256,256]{2,1,0:T(8,128)(2,1)S(1)} %get-tuple-element.33.probs_ref, bf16[3,256,256]{2,1,0:T(8,128)(2,1)S(1)} %get-tuple-element.34.dscores_ref, ...), custom_call_target="tpu_custom_call" | custom-call | tf_op jit(solution)/shard_map/terms/pallas_call | solution.py:260
  20.0 2.5 %collective-permute-start.7 = (bf16[64,768]{1,0:T(8,128)(2,1)S(1)}, bf16[64,768]{1,0:T(8,128)(2,1)S(1)}, u32[]{:S(2)}, u32[]{:S(2)}) collective-permute-start(bf16[64,768]{1,0:T(8,128)(2,1)S(1)} %get-tuple-element.36), channel_id=1, source_target_pairs={{0,6},{2,4},{4,2},{6,0},{1,7},{3,5},{5,3},{7,1},{8,14},{10,12},{12... | collective-permute-start | bytes 294920 | tf_op jit(solution)/shard_map/ppermute | solution.py:26
  22.5 0.6 %collective-permute-start.8 = (bf16[64,768]{1,0:T(8,128)(2,1)S(1)}, bf16[64,768]{1,0:T(8,128)(2,1)S(1)}, u32[]{:S(2)}, u32[]{:S(2)}) collective-permute-start(bf16[64,768]{1,0:T(8,128)(2,1)S(1)} %get-tuple-element.37), channel_id=1, source_target_pairs={{0,4},{2,6},{4,0},{6,2},{1,5},{3,7},{5,1},{7,3},{8,12},{10,14},{12... | collective-permute-start | bytes 294920 | tf_op jit(solution)/shard_map/ppermute | solution.py:26
  23.1 1.3 %collective-permute-start.9 = (bf16[64,768]{1,0:T(8,128)(2,1)S(1)}, bf16[64,768]{1,0:T(8,128)(2,1)S(1)}, u32[]{:S(2)}, u32[]{:S(2)}) collective-permute-start(bf16[64,768]{1,0:T(8,128)(2,1)S(1)} %get-tuple-element.38), channel_id=1, source_target_pairs={{0,2},{2,0},{4,6},{6,4},{1,3},{3,1},{5,7},{7,5},{8,10},{10,8},{12,... | collective-permute-start | bytes 294920 | tf_op jit(solution)/shard_map/ppermute | solution.py:26
  24.5 3.4 %own.1.own_ref = f32[2688,128]{1,0:T(8,128)S(1)} custom-call(bf16[768,128]{1,0:T(8,128)(2,1)S(1)} %get-tuple-element.31.grad_ref, bf16[1,5376,768]{2,1,0:T(8,128)(2,1)} %w_ref.3), custom_call_target="tpu_custom_call" | custom-call | tf_op jit(solution)/shard_map/own/pallas_call | solution.py:269
  27.9 0.0 collective-permute-done.7.refs_1_
  27.9 2.4 %collective-permute-done.8.refs_2_ = bf16[64,768]{1,0:T(8,128)(2,1)S(1)} collective-permute-done((bf16[64,768]{1,0:T(8,128)(2,1)S(1)}, bf16[64,768]{1,0:T(8,128)(2,1)S(1)}, u32[]{:S(2)}, u32[]{:S(2)}) %collective-permute-start.8) | collective-permute-done | bytes 98336 | tf_op jit(solution)/shard_map/ppermute | solution.py:26
  30.3 0.0 collective-permute-done.9.refs_3_
  30.3 0.7 %term_sum.1 = (bf16[1,64,384]{2,1,0:T(8,128)(2,1)}, bf16[1,64,384]{2,1,0:T(8,128)(2,1)}) custom-call(bf16[64,768]{1,0:T(8,128)(2,1)S(1)} %get-tuple-element.35.refs_0_, bf16[64,768]{1,0:T(8,128)(2,1)S(1)} %collective-permute-done.7.refs_1_, bf16[64,768]{1,0:T(8,128)(2,1)S(1)} %collective-permute-done.8.refs_2_, ...), custom_call_target="tpu_custom_call" | custom-call | tf_op jit(solution)/shard_map/term_sum/pallas_call | solution.py:276
  31.0 0.0 collective-permute-done.6.refs_0_
  31.0 0.8 %input_sum.2.refs_1_ = bf16[1,2688,128]{2,1,0:T(8,128)(2,1)} custom-call(f32[2688,128]{1,0:T(8,128)S(1)} %own.1.own_ref, bf16[1424,128]{1,0:T(8,128)(2,1)S(1)} %collective-permute-done.6.refs_0_), custom_call_target="tpu_custom_call" | custom-call | tf_op jit(solution)/shard_map/input_sum/pallas_call | solution.py:282
  31.8 0.4 %collective-permute-done.5.refs_0_ = bf16[1264,128]{1,0:T(8,128)(2,1)S(1)} collective-permute-done((bf16[1264,128]{1,0:T(8,128)(2,1)S(1)}, bf16[1264,128]{1,0:T(8,128)(2,1)S(1)}, u32[]{:S(2)}, u32[]{:S(2)}) %collective-permute-start.5) | collective-permute-done | bytes 323616 | tf_op jit(solution)/shard_map/ppermute | solution.py:22
  32.2 0.8 %input_sum.3 = bf16[1,2688,128]{2,1,0:T(8,128)(2,1)} custom-call(f32[2688,128]{1,0:T(8,128)S(1)} %own.1.own_ref, bf16[1264,128]{1,0:T(8,128)(2,1)S(1)} %collective-permute-done.5.refs_0_, bf16[1,2688,128]{2,1,0:T(8,128)(2,1)} %input_sum.2.refs_1_), custom_call_target="tpu_custom_call", output_to_operand_aliasing={{}: (2, {})} | custom-call | tf_op jit(solution)/shard_map/input_sum/pallas_call | solution.py:282
Async XLA Ops:
  1.7 9.7 %collective-permute-start = (bf16[64,768]{1,0:T(8,128)(2,1)S(1)}, bf16[64,768]{1,0:T(8,128)(2,1)S(1)}, u32[]{:S(2)}, u32[]{:S(2)}) collective-permute-start(bf16[64,768]{1,0:T(8,128)(2,1)S(1)} %get-tuple-element.25), channel_id=1, source_target_pairs={{0,2},{2,0},{4,6},{6,4},{1,3},{3,1},{5,7},{7,5},{8,10},{10,8},{12,... | collective-permute-start | bytes 294920 | tf_op jit(solution)/shard_map/ppermute | solution.py:26
  4.8 10.4 %collective-permute-start.1 = (bf16[64,768]{1,0:T(8,128)(2,1)S(1)}, bf16[64,768]{1,0:T(8,128)(2,1)S(1)}, u32[]{:S(2)}, u32[]{:S(2)}) collective-permute-start(bf16[64,768]{1,0:T(8,128)(2,1)S(1)} %get-tuple-element.26), channel_id=1, source_target_pairs={{0,4},{2,6},{4,0},{6,2},{1,5},{3,7},{5,1},{7,3},{8,12},{10,14},{12... | collective-permute-start | bytes 294920 | tf_op jit(solution)/shard_map/ppermute | solution.py:26
  7.4 7.8 %collective-permute-start.2 = (bf16[64,768]{1,0:T(8,128)(2,1)S(1)}, bf16[64,768]{1,0:T(8,128)(2,1)S(1)}, u32[]{:S(2)}, u32[]{:S(2)}) collective-permute-start(bf16[64,768]{1,0:T(8,128)(2,1)S(1)} %get-tuple-element.27), channel_id=1, source_target_pairs={{0,6},{2,4},{4,2},{6,0},{1,7},{3,5},{5,3},{7,1},{8,14},{10,12},{12... | collective-permute-start | bytes 294920 | tf_op jit(solution)/shard_map/ppermute | solution.py:26
  7.4 7.8 %collective-permute-start.3 = (bf16[64,768]{1,0:T(8,128)(2,1)S(1)}, bf16[64,768]{1,0:T(8,128)(2,1)S(1)}, u32[]{:S(2)}, u32[]{:S(2)}) collective-permute-start(bf16[64,768]{1,0:T(8,128)(2,1)S(1)} %get-tuple-element.28), channel_id=1, source_target_pairs={{8,0},{16,8},{24,16},{0,24},{9,1},{17,9},{25,17},{1,25},{10,2},{18... | collective-permute-start | bytes 294920 | tf_op jit(solution)/shard_map/ppermute | solution.py:22
  7.7 7.5 %collective-permute-start.4 = (bf16[64,768]{1,0:T(8,128)(2,1)S(1)}, bf16[64,768]{1,0:T(8,128)(2,1)S(1)}, u32[]{:S(2)}, u32[]{:S(2)}) collective-permute-start(bf16[64,768]{1,0:T(8,128)(2,1)S(1)} %get-tuple-element.29), channel_id=1, source_target_pairs={{8,0},{16,8},{24,16},{0,24},{9,1},{17,9},{25,17},{1,25},{10,2},{18... | collective-permute-start | bytes 294920 | tf_op jit(solution)/shard_map/ppermute | solution.py:22
  16.8 14.2 %collective-permute-start.6 = (bf16[1424,128]{1,0:T(8,128)(2,1)S(1)}, bf16[1424,128]{1,0:T(8,128)(2,1)S(1)}, u32[]{:S(2)}, u32[]{:S(2)}) collective-permute-start(bf16[1424,128]{1,0:T(8,128)(2,1)S(1)} %get-tuple-element.32), channel_id=1, source_target_pairs={{1,0},{0,1},{3,2},{2,3},{5,4},{4,5},{7,6},{6,7},{9,8},{8,9},{11,10... | collective-permute-start | bytes 1093640 | tf_op jit(solution)/shard_map/ppermute | solution.py:22
  19.1 13.1 %collective-permute-start.5 = (bf16[1264,128]{1,0:T(8,128)(2,1)S(1)}, bf16[1264,128]{1,0:T(8,128)(2,1)S(1)}, u32[]{:S(2)}, u32[]{:S(2)}) collective-permute-start(bf16[1264,128]{1,0:T(8,128)(2,1)S(1)} %rest.1), channel_id=1, source_target_pairs={{1,0},{0,1},{3,2},{2,3},{5,4},{4,5},{7,6},{6,7},{9,8},{8,9},{11,10... | collective-permute-start | bytes 970760 | tf_op jit(solution)/shard_map/ppermute | solution.py:22
  20.0 7.9 %collective-permute-start.7 = (bf16[64,768]{1,0:T(8,128)(2,1)S(1)}, bf16[64,768]{1,0:T(8,128)(2,1)S(1)}, u32[]{:S(2)}, u32[]{:S(2)}) collective-permute-start(bf16[64,768]{1,0:T(8,128)(2,1)S(1)} %get-tuple-element.36), channel_id=1, source_target_pairs={{0,6},{2,4},{4,2},{6,0},{1,7},{3,5},{5,3},{7,1},{8,14},{10,12},{12... | collective-permute-start | bytes 294920 | tf_op jit(solution)/shard_map/ppermute | solution.py:26
  22.5 7.7 %collective-permute-start.8 = (bf16[64,768]{1,0:T(8,128)(2,1)S(1)}, bf16[64,768]{1,0:T(8,128)(2,1)S(1)}, u32[]{:S(2)}, u32[]{:S(2)}) collective-permute-start(bf16[64,768]{1,0:T(8,128)(2,1)S(1)} %get-tuple-element.37), channel_id=1, source_target_pairs={{0,4},{2,6},{4,0},{6,2},{1,5},{3,7},{5,1},{7,3},{8,12},{10,14},{12... | collective-permute-start | bytes 294920 | tf_op jit(solution)/shard_map/ppermute | solution.py:26
  23.1 7.1 %collective-permute-start.9 = (bf16[64,768]{1,0:T(8,128)(2,1)S(1)}, bf16[64,768]{1,0:T(8,128)(2,1)S(1)}, u32[]{:S(2)}, u32[]{:S(2)}) collective-permute-start(bf16[64,768]{1,0:T(8,128)(2,1)S(1)} %get-tuple-element.38), channel_id=1, source_target_pairs={{0,2},{2,0},{4,6},{6,4},{1,3},{3,1},{5,7},{7,5},{8,10},{10,8},{12,... | collective-permute-start | bytes 294920 | tf_op jit(solution)/shard_map/ppermute | solution.py:26

commit v4 on v3

--- a/solution.py
+++ b/solution.py
@@ -162,15 +162,21 @@
 
 def input_sum_kernel(n_other, start, own_ref, *refs):
     arrived = refs[:n_other]
-    *_, out_ref, held, sem = refs
-    at = slice(start, start + held.shape[0])
-    total = own_ref[at, :]
-    for ref in arrived:
-        total = total + ref[...].astype(jnp.float32)
-    held[...] = total.astype(jnp.bfloat16)
-    copy = pltpu.make_async_copy(held, out_ref.at[0, at, :], sem)
-    copy.start()
-    copy.wait()
+    *_, out_ref, held, sems = refs
+    count = held.shape[0]
+    middle = count // 32 * 16
+    copies = []
+    for i, (low, high) in enumerate(((0, middle), (middle, count))):
+        at = slice(start + low, start + high)
+        total = own_ref[at, :]
+        for ref in arrived:
+            total = total + ref[low:high, :].astype(jnp.float32)
+        held[low:high, :] = total.astype(jnp.bfloat16)
+        copy = pltpu.make_async_copy(held.at[low:high, :], out_ref.at[0, at, :], sems.at[i])
+        copy.start()
+        copies.append(copy)
+    for copy in copies:
+        copy.wait()
 
 
 def term_sum_kernel(*refs):
@@ -261,7 +267,7 @@
         terms_kernel, "terms", [shape(block_rows, 2 * kv_width)] * n_blocks, [VMEM] * 5
     )(probs, dscores, q, *incoming)
     if direct:
-        sent = sorted(zip(partners, terms[1:]), key=lambda pair: -pair[0])
+        sent = sorted(zip(partners, terms[1:]), key=lambda pair: -pair[0].bit_length())
         all_terms = [terms[0]] + [swapped(x, "seq", r) for r, x in sent]
     else:
         all_terms = [lax.psum_scatter(terms[0], "seq", scatter_dimension=0, tiled=True)]
@@ -284,7 +290,7 @@
                 out_shape=shape(1, feats, rows),
                 in_specs=[VMEM] * (1 + n_other) + [HBM] * len(grad_input),
                 out_specs=HBM,
-                scratch_shapes=[pltpu.VMEM(part[0].shape, low), pltpu.SemaphoreType.DMA(())],
+                scratch_shapes=[pltpu.VMEM(part[0].shape, low), pltpu.SemaphoreType.DMA((2,))],
                 input_output_aliases={1 + n_other: 0} if grad_input else {},
                 compiler_params=pltpu.CompilerParams(vmem_limit_bytes=VMEM_LIMIT),
                 name="input_sum",

time: 33.1 us -> 33.1 us (level)
  waiting for transfers between devices: 6.57 us -> 7.02 us
  starting transfers between devices: 14.1 us -> 13.7 us
    ppermute x6, starting transfers between devices: 10.1 us -> 9.72 us  [swapped(): lax.ppermute(block, axis, [(i, i ^ distance) for i in range(lax.axis_size...]
  transfers between devices with their start and end apart: 10 -> 10, of which waited for: 3 -> 5; matrix products, arithmetic and copies ran while one was open for 0% -> 0% of each run, Pallas kernels for 25% -> 25%
where the time goes in v4:
time: 33.1 us; the launch traced here: 32.9 us
  starting transfers between devices  13.7 us (41%)
  Pallas kernels  11.5 us (35%)
  waiting for transfers between devices  7.02 us (21%)
  between operations  0.7 us (2%)
    ppermute x6, starting transfers between devices, swapped(): lax.ppermute(block, axis, [(i, i ^ distance) for i in range(lax.axis_size...  9.72 us
    ppermute x6, waiting for transfers between devices, swapped(): lax.ppermute(block, axis, [(i, i ^ distance) for i in range(lax.axis_size...  6.36 us
    ppermute x4, starting transfers between devices, shifted(): return lax.ppermute(block, axis, route)  3.98 us
    pallas_call x1, Pallas kernels, on_device(): kernel_call(functools.partial(own_kernel, n_head), 'own', shape(feats, ro...  3.41 us
    pallas_call x1, Pallas kernels, on_device(): kernel_call(functools.partial(stage_kernel, n_head), 'stage', [shape(8, H...  2.21 us
    pallas_call x1, Pallas kernels, on_device(): kernel_call(functools.partial(attention_kernel, partners, n_other), 'atte...  1.6 us
    pallas_call x2, Pallas kernels, on_device(): pl.pallas_call(functools.partial(input_sum_kernel, n_other, start), out_s...  1.55 us
    pallas_call x1, Pallas kernels, on_device(): kernel_call(functools.partial(join_kernel, n_copies), 'join', [shape(held...  1.04 us
  transfers between devices with their start and end apart: 10, of which 5 were waited for; matrix products, arithmetic and copies ran while one was open for 0% of the time, Pallas kernels for 25%

profile of v4, /device:TPU:0, one launch (start us, length us, event | category | flops | bytes accessed | tf_op | source)
XLA Modules:
  0.0 32.9 jit_solution(1112749778732045666)
XLA Ops:
  0.6 1.0 %join.1 = (bf16[64,768]{1,0:T(8,128)(2,1)S(1)}, bf16[64,768]{1,0:T(8,128)(2,1)S(1)}, bf16[64,768]{1,0:T(8,128)(2,1)S(1)}, bf16[64,768]{1,0:T(8,128)(2,1)S(1)}, b...) custom-call(bf16[1,64,384]{2,1,0:T(8,128)(2,1)} %key_ref.1, bf16[1,64,384]{2,1,0:T(8,128)(2,1)} %value_ref.1, ...), custom_call_target="tpu_custom_call" | custom-call | tf_op jit(solution)/shard_map/join/pallas_call | solution.py:224
  1.7 3.1 %collective-permute-start = (bf16[64,768]{1,0:T(8,128)(2,1)S(1)}, bf16[64,768]{1,0:T(8,128)(2,1)S(1)}, u32[]{:S(2)}, u32[]{:S(2)}) collective-permute-start(bf16[64,768]{1,0:T(8,128)(2,1)S(1)} %get-tuple-element.25), channel_id=1, source_target_pairs={{0,2},{2,0},{4,6},{6,4},{1,3},{3,1},{5,7},{7,5},{8,10},{10,8},{12,... | collective-permute-start | bytes 294920 | tf_op jit(solution)/shard_map/ppermute | solution.py:26
  4.8 2.6 %collective-permute-start.1 = (bf16[64,768]{1,0:T(8,128)(2,1)S(1)}, bf16[64,768]{1,0:T(8,128)(2,1)S(1)}, u32[]{:S(2)}, u32[]{:S(2)}) collective-permute-start(bf16[64,768]{1,0:T(8,128)(2,1)S(1)} %get-tuple-element.26), channel_id=1, source_target_pairs={{0,4},{2,6},{4,0},{6,2},{1,5},{3,7},{5,1},{7,3},{8,12},{10,14},{12... | collective-permute-start | bytes 294920 | tf_op jit(solution)/shard_map/ppermute | solution.py:26
  7.4 0.0 collective-permute-start.2
  7.4 0.4 %collective-permute-start.3 = (bf16[64,768]{1,0:T(8,128)(2,1)S(1)}, bf16[64,768]{1,0:T(8,128)(2,1)S(1)}, u32[]{:S(2)}, u32[]{:S(2)}) collective-permute-start(bf16[64,768]{1,0:T(8,128)(2,1)S(1)} %get-tuple-element.28), channel_id=1, source_target_pairs={{8,0},{16,8},{24,16},{0,24},{9,1},{17,9},{25,17},{1,25},{10,2},{18... | collective-permute-start | bytes 294920 | tf_op jit(solution)/shard_map/ppermute | solution.py:22
  7.7 1.5 %collective-permute-start.4 = (bf16[64,768]{1,0:T(8,128)(2,1)S(1)}, bf16[64,768]{1,0:T(8,128)(2,1)S(1)}, u32[]{:S(2)}, u32[]{:S(2)}) collective-permute-start(bf16[64,768]{1,0:T(8,128)(2,1)S(1)} %get-tuple-element.29), channel_id=1, source_target_pairs={{8,0},{16,8},{24,16},{0,24},{9,1},{17,9},{25,17},{1,25},{10,2},{18... | collective-permute-start | bytes 294920 | tf_op jit(solution)/shard_map/ppermute | solution.py:22
  9.2 2.2 %stage.1 = (s32[8,128]{1,0:T(8,128)S(1)}, bf16[128,768]{1,0:T(8,128)(2,1)S(1)}, bf16[2688,768]{1,0:T(8,128)(2,1)S(1)}) custom-call(s32[4]{0:T(128)} %span_ref.1, s32[4]{0:T(128)} %prefix_ref.1, bf16[1,128,768]{2,1,0:T(8,128)(2,1)} %q_ref.1, bf16[1,5376,768]{2,1,0:T(8,128)(2,1)} %w_ref.3), custom_call_target="tpu_custom_call" | custom-call | tf_op jit(solution)/shard_map/stage/pallas_call | solution.py:238
  11.4 0.0 collective-permute-done.refs_1_
  11.4 3.8 %collective-permute-done.1.refs_2_ = bf16[64,768]{1,0:T(8,128)(2,1)S(1)} collective-permute-done((bf16[64,768]{1,0:T(8,128)(2,1)S(1)}, bf16[64,768]{1,0:T(8,128)(2,1)S(1)}, u32[]{:S(2)}, u32[]{:S(2)}) %collective-permute-start.1) | collective-permute-done | bytes 98336 | tf_op jit(solution)/shard_map/ppermute | solution.py:26
  15.2 0.0 collective-permute-done.2.refs_3_
  15.2 0.0 collective-permute-done.3.refs_4_.d_low
  15.2 0.0 collective-permute-done.4.refs_5_.d_high
  15.2 1.6 %attention.1 = (bf16[768,128]{1,0:T(8,128)(2,1)S(1)}, bf16[3,256,256]{2,1,0:T(8,128)(2,1)S(1)}, bf16[3,256,256]{2,1,0:T(8,128)(2,1)S(1)}, bf16[1424,128]{1,0:T(8,128)(2,1)S(1)}) custom-call(s32[8,128]{1,0:T(8,128)S(1)} %get-tuple-element.22.limit_ref, bf16[128,768]{1,0:T(8,128)(2,1)S(1)} %get-tuple-element.23.q_ref, ...), custom_call_target="tpu_custom_call" | custom-call | tf_op jit(solution)/shard_map/attention/pallas_call | solution.py:253
  16.8 1.6 %collective-permute-start.6 = (bf16[1424,128]{1,0:T(8,128)(2,1)S(1)}, bf16[1424,128]{1,0:T(8,128)(2,1)S(1)}, u32[]{:S(2)}, u32[]{:S(2)}) collective-permute-start(bf16[1424,128]{1,0:T(8,128)(2,1)S(1)} %get-tuple-element.32), channel_id=1, source_target_pairs={{1,0},{0,1},{3,2},{2,3},{5,4},{4,5},{7,6},{6,7},{9,8},{8,9},{11,10... | collective-permute-start | bytes 1093640 | tf_op jit(solution)/shard_map/ppermute | solution.py:22
  18.4 0.7 %rest.1 = bf16[1264,128]{1,0:T(8,128)(2,1)S(1)} custom-call(bf16[768,128]{1,0:T(8,128)(2,1)S(1)} %get-tuple-element.31.grad_ref, bf16[2688,768]{1,0:T(8,128)(2,1)S(1)} %get-tuple-element.30.refs_6_.refs_0_), custom_call_target="tpu_custom_call" | custom-call | tf_op jit(solution)/shard_map/rest/pallas_call | solution.py:259
  19.1 0.6 %collective-permute-start.5 = (bf16[1264,128]{1,0:T(8,128)(2,1)S(1)}, bf16[1264,128]{1,0:T(8,128)(2,1)S(1)}, u32[]{:S(2)}, u32[]{:S(2)}) collective-permute-start(bf16[1264,128]{1,0:T(8,128)(2,1)S(1)} %rest.1), channel_id=1, source_target_pairs={{1,0},{0,1},{3,2},{2,3},{5,4},{4,5},{7,6},{6,7},{9,8},{8,9},{11,10... | collective-permute-start | bytes 970760 | tf_op jit(solution)/shard_map/ppermute | solution.py:22
  19.6 0.4 %terms.1 = (bf16[64,768]{1,0:T(8,128)(2,1)S(1)}, bf16[64,768]{1,0:T(8,128)(2,1)S(1)}, bf16[64,768]{1,0:T(8,128)(2,1)S(1)}, bf16[64,768]{1,0:T(8,128)(2,1)S(1)}) custom-call(bf16[3,256,256]{2,1,0:T(8,128)(2,1)S(1)} %get-tuple-element.33.probs_ref, bf16[3,256,256]{2,1,0:T(8,128)(2,1)S(1)} %get-tuple-element.34.dscores_ref, ...), custom_call_target="tpu_custom_call" | custom-call | tf_op jit(solution)/shard_map/terms/pallas_call | solution.py:266
  20.0 2.7 %collective-permute-start.7 = (bf16[64,768]{1,0:T(8,128)(2,1)S(1)}, bf16[64,768]{1,0:T(8,128)(2,1)S(1)}, u32[]{:S(2)}, u32[]{:S(2)}) collective-permute-start(bf16[64,768]{1,0:T(8,128)(2,1)S(1)} %get-tuple-element.36), channel_id=1, source_target_pairs={{0,4},{2,6},{4,0},{6,2},{1,5},{3,7},{5,1},{7,3},{8,12},{10,14},{12... | collective-permute-start | bytes 294920 | tf_op jit(solution)/shard_map/ppermute | solution.py:26
  22.7 1.3 %collective-permute-start.8 = (bf16[64,768]{1,0:T(8,128)(2,1)S(1)}, bf16[64,768]{1,0:T(8,128)(2,1)S(1)}, u32[]{:S(2)}, u32[]{:S(2)}) collective-permute-start(bf16[64,768]{1,0:T(8,128)(2,1)S(1)} %get-tuple-element.37), channel_id=1, source_target_pairs={{0,6},{2,4},{4,2},{6,0},{1,7},{3,5},{5,3},{7,1},{8,14},{10,12},{12... | collective-permute-start | bytes 294920 | tf_op jit(solution)/shard_map/ppermute | solution.py:26
  24.0 0.0 collective-permute-start.9
  24.0 3.4 %own.1.own_ref = f32[2688,128]{1,0:T(8,128)S(1)} custom-call(bf16[768,128]{1,0:T(8,128)(2,1)S(1)} %get-tuple-element.31.grad_ref, bf16[1,5376,768]{2,1,0:T(8,128)(2,1)} %w_ref.3), custom_call_target="tpu_custom_call" | custom-call | tf_op jit(solution)/shard_map/own/pallas_call | solution.py:275
  27.5 0.5 %collective-permute-done.7.refs_1_ = bf16[64,768]{1,0:T(8,128)(2,1)S(1)} collective-permute-done((bf16[64,768]{1,0:T(8,128)(2,1)S(1)}, bf16[64,768]{1,0:T(8,128)(2,1)S(1)}, u32[]{:S(2)}, u32[]{:S(2)}) %collective-permute-start.7) | collective-permute-done | bytes 98336 | tf_op jit(solution)/shard_map/ppermute | solution.py:26
  28.0 1.2 %collective-permute-done.8.refs_2_ = bf16[64,768]{1,0:T(8,128)(2,1)S(1)} collective-permute-done((bf16[64,768]{1,0:T(8,128)(2,1)S(1)}, bf16[64,768]{1,0:T(8,128)(2,1)S(1)}, u32[]{:S(2)}, u32[]{:S(2)}) %collective-permute-start.8) | collective-permute-done | bytes 98336 | tf_op jit(solution)/shard_map/ppermute | solution.py:26
  29.3 0.8 %collective-permute-done.9.refs_3_ = bf16[64,768]{1,0:T(8,128)(2,1)S(1)} collective-permute-done((bf16[64,768]{1,0:T(8,128)(2,1)S(1)}, bf16[64,768]{1,0:T(8,128)(2,1)S(1)}, u32[]{:S(2)}, u32[]{:S(2)}) %collective-permute-start.9) | collective-permute-done | bytes 98336 | tf_op jit(solution)/shard_map/ppermute | solution.py:26
  30.0 0.7 %term_sum.1 = (bf16[1,64,384]{2,1,0:T(8,128)(2,1)}, bf16[1,64,384]{2,1,0:T(8,128)(2,1)}) custom-call(bf16[64,768]{1,0:T(8,128)(2,1)S(1)} %get-tuple-element.35.refs_0_, bf16[64,768]{1,0:T(8,128)(2,1)S(1)} %collective-permute-done.7.refs_1_, bf16[64,768]{1,0:T(8,128)(2,1)S(1)} %collective-permute-done.8.refs_2_, ...), custom_call_target="tpu_custom_call" | custom-call | tf_op jit(solution)/shard_map/term_sum/pallas_call | solution.py:282
  30.7 0.0 collective-permute-done.6.refs_0_
  30.7 0.8 %input_sum.2.refs_1_ = bf16[1,2688,128]{2,1,0:T(8,128)(2,1)} custom-call(f32[2688,128]{1,0:T(8,128)S(1)} %own.1.own_ref, bf16[1424,128]{1,0:T(8,128)(2,1)S(1)} %collective-permute-done.6.refs_0_), custom_call_target="tpu_custom_call" | custom-call | tf_op jit(solution)/shard_map/input_sum/pallas_call | solution.py:288
  31.5 0.7 %collective-permute-done.5.refs_0_ = bf16[1264,128]{1,0:T(8,128)(2,1)S(1)} collective-permute-done((bf16[1264,128]{1,0:T(8,128)(2,1)S(1)}, bf16[1264,128]{1,0:T(8,128)(2,1)S(1)}, u32[]{:S(2)}, u32[]{:S(2)}) %collective-permute-start.5) | collective-permute-done | bytes 323616 | tf_op jit(solution)/shard_map/ppermute | solution.py:22
  32.2 0.8 %input_sum.3 = bf16[1,2688,128]{2,1,0:T(8,128)(2,1)} custom-call(f32[2688,128]{1,0:T(8,128)S(1)} %own.1.own_ref, bf16[1264,128]{1,0:T(8,128)(2,1)S(1)} %collective-permute-done.5.refs_0_, bf16[1,2688,128]{2,1,0:T(8,128)(2,1)} %input_sum.2.refs_1_), custom_call_target="tpu_custom_call", output_to_operand_aliasing={{}: (2, {})} | custom-call | tf_op jit(solution)/shard_map/input_sum/pallas_call | solution.py:288
Async XLA Ops:
  1.7 9.7 %collective-permute-start = (bf16[64,768]{1,0:T(8,128)(2,1)S(1)}, bf16[64,768]{1,0:T(8,128)(2,1)S(1)}, u32[]{:S(2)}, u32[]{:S(2)}) collective-permute-start(bf16[64,768]{1,0:T(8,128)(2,1)S(1)} %get-tuple-element.25), channel_id=1, source_target_pairs={{0,2},{2,0},{4,6},{6,4},{1,3},{3,1},{5,7},{7,5},{8,10},{10,8},{12,... | collective-permute-start | bytes 294920 | tf_op jit(solution)/shard_map/ppermute | solution.py:26
  4.8 10.4 %collective-permute-start.1 = (bf16[64,768]{1,0:T(8,128)(2,1)S(1)}, bf16[64,768]{1,0:T(8,128)(2,1)S(1)}, u32[]{:S(2)}, u32[]{:S(2)}) collective-permute-start(bf16[64,768]{1,0:T(8,128)(2,1)S(1)} %get-tuple-element.26), channel_id=1, source_target_pairs={{0,4},{2,6},{4,0},{6,2},{1,5},{3,7},{5,1},{7,3},{8,12},{10,14},{12... | collective-permute-start | bytes 294920 | tf_op jit(solution)/shard_map/ppermute | solution.py:26
  7.4 7.8 %collective-permute-start.2 = (bf16[64,768]{1,0:T(8,128)(2,1)S(1)}, bf16[64,768]{1,0:T(8,128)(2,1)S(1)}, u32[]{:S(2)}, u32[]{:S(2)}) collective-permute-start(bf16[64,768]{1,0:T(8,128)(2,1)S(1)} %get-tuple-element.27), channel_id=1, source_target_pairs={{0,6},{2,4},{4,2},{6,0},{1,7},{3,5},{5,3},{7,1},{8,14},{10,12},{12... | collective-permute-start | bytes 294920 | tf_op jit(solution)/shard_map/ppermute | solution.py:26
  7.4 7.8 %collective-permute-start.3 = (bf16[64,768]{1,0:T(8,128)(2,1)S(1)}, bf16[64,768]{1,0:T(8,128)(2,1)S(1)}, u32[]{:S(2)}, u32[]{:S(2)}) collective-permute-start(bf16[64,768]{1,0:T(8,128)(2,1)S(1)} %get-tuple-element.28), channel_id=1, source_target_pairs={{8,0},{16,8},{24,16},{0,24},{9,1},{17,9},{25,17},{1,25},{10,2},{18... | collective-permute-start | bytes 294920 | tf_op jit(solution)/shard_map/ppermute | solution.py:22
  7.7 7.5 %collective-permute-start.4 = (bf16[64,768]{1,0:T(8,128)(2,1)S(1)}, bf16[64,768]{1,0:T(8,128)(2,1)S(1)}, u32[]{:S(2)}, u32[]{:S(2)}) collective-permute-start(bf16[64,768]{1,0:T(8,128)(2,1)S(1)} %get-tuple-element.29), channel_id=1, source_target_pairs={{8,0},{16,8},{24,16},{0,24},{9,1},{17,9},{25,17},{1,25},{10,2},{18... | collective-permute-start | bytes 294920 | tf_op jit(solution)/shard_map/ppermute | solution.py:22
  16.8 13.9 %collective-permute-start.6 = (bf16[1424,128]{1,0:T(8,128)(2,1)S(1)}, bf16[1424,128]{1,0:T(8,128)(2,1)S(1)}, u32[]{:S(2)}, u32[]{:S(2)}) collective-permute-start(bf16[1424,128]{1,0:T(8,128)(2,1)S(1)} %get-tuple-element.32), channel_id=1, source_target_pairs={{1,0},{0,1},{3,2},{2,3},{5,4},{4,5},{7,6},{6,7},{9,8},{8,9},{11,10... | collective-permute-start | bytes 1093640 | tf_op jit(solution)/shard_map/ppermute | solution.py:22
  19.1 13.1 %collective-permute-start.5 = (bf16[1264,128]{1,0:T(8,128)(2,1)S(1)}, bf16[1264,128]{1,0:T(8,128)(2,1)S(1)}, u32[]{:S(2)}, u32[]{:S(2)}) collective-permute-start(bf16[1264,128]{1,0:T(8,128)(2,1)S(1)} %rest.1), channel_id=1, source_target_pairs={{1,0},{0,1},{3,2},{2,3},{5,4},{4,5},{7,6},{6,7},{9,8},{8,9},{11,10... | collective-permute-start | bytes 970760 | tf_op jit(solution)/shard_map/ppermute | solution.py:22
  20.0 8.0 %collective-permute-start.7 = (bf16[64,768]{1,0:T(8,128)(2,1)S(1)}, bf16[64,768]{1,0:T(8,128)(2,1)S(1)}, u32[]{:S(2)}, u32[]{:S(2)}) collective-permute-start(bf16[64,768]{1,0:T(8,128)(2,1)S(1)} %get-tuple-element.36), channel_id=1, source_target_pairs={{0,4},{2,6},{4,0},{6,2},{1,5},{3,7},{5,1},{7,3},{8,12},{10,14},{12... | collective-permute-start | bytes 294920 | tf_op jit(solution)/shard_map/ppermute | solution.py:26
  22.7 6.6 %collective-permute-start.8 = (bf16[64,768]{1,0:T(8,128)(2,1)S(1)}, bf16[64,768]{1,0:T(8,128)(2,1)S(1)}, u32[]{:S(2)}, u32[]{:S(2)}) collective-permute-start(bf16[64,768]{1,0:T(8,128)(2,1)S(1)} %get-tuple-element.37), channel_id=1, source_target_pairs={{0,6},{2,4},{4,2},{6,0},{1,7},{3,5},{5,3},{7,1},{8,14},{10,12},{12... | collective-permute-start | bytes 294920 | tf_op jit(solution)/shard_map/ppermute | solution.py:26
  24.0 6.0 %collective-permute-start.9 = (bf16[64,768]{1,0:T(8,128)(2,1)S(1)}, bf16[64,768]{1,0:T(8,128)(2,1)S(1)}, u32[]{:S(2)}, u32[]{:S(2)}) collective-permute-start(bf16[64,768]{1,0:T(8,128)(2,1)S(1)} %get-tuple-element.38), channel_id=1, source_target_pairs={{0,2},{2,0},{4,6},{6,4},{1,3},{3,1},{5,7},{7,5},{8,10},{10,8},{12,... | collective-permute-start | bytes 294920 | tf_op jit(solution)/shard_map/ppermute | solution.py:26

commit v5 on v3

--- a/solution.py
+++ b/solution.py
@@ -90,9 +90,10 @@
 
 
 def attention_kernel(partners, n_other, limit_ref, q_ref, *refs):
-    n_blocks = 1 + len(partners)
-    kv_refs = refs[:n_blocks]
-    d_low, d_high, *refs = refs[n_blocks:]
+    most = 1 + len(partners[:-1])
+    kv_refs, (d_low, d_high), refs = refs[:most], refs[most : most + 2], refs[most + 2 :]
+    if partners:
+        kv_refs, refs = kv_refs + refs[:1], refs[1:]
     w_refs = refs[:n_other]
     grad_ref, probs_ref, dscores_ref, *part_refs = refs[n_other:]
 
@@ -223,11 +224,12 @@
         [pltpu.SemaphoreType.DMA((4,))],
     )(*[in_hbm(x) for x in (keys, values, grad_out)])
     if direct:
-        blocks = joined[-1:] + [swapped(x, "seq", r) for x, r in zip(joined, partners)]
+        blocks = joined[-1:] + [swapped(x, "seq", r) for x, r in zip(joined, partners[:-1])]
     else:
         blocks = [lax.all_gather(joined[0], "seq", axis=0, tiled=True)]
-    n_blocks, block_rows = len(blocks), blocks[0].shape[0]
     incoming = [shifted(part, "section", -1) for part in (grad_low, grad_high)]
+    last = [swapped(joined[len(partners) - 1], "seq", r) for r in partners[-1:]]
+    n_blocks, block_rows = len(blocks) + len(last), blocks[0].shape[0]
 
     limit, q, *w_other = kernel_call(
         functools.partial(stage_kernel, n_head),
@@ -249,7 +251,7 @@
         "attention",
         [shape(width, rows), weights, weights] + [shape(first, rows)] * n_other,
         [VMEM] * (4 + n_blocks + n_other),
-    )(limit, q, *blocks, *incoming, *w_other)
+    )(limit, q, *blocks, *incoming, *last, *w_other)
     rest = kernel_call(
         functools.partial(rest_kernel, n_other),
         "rest",

time: 33.1 us -> 33.6 us (1.015)
  waiting for transfers between devices: 6.57 us -> 7.02 us
    ppermute x6, waiting for transfers between devices: 6.17 us -> 6.63 us  [swapped(): lax.ppermute(block, axis, [(i, i ^ distance) for i in range(lax.axis_size...]
  transfers between devices with their start and end apart: 10 -> 10, of which waited for: 3 -> 4; matrix products, arithmetic and copies ran while one was open for 0% -> 0% of each run, Pallas kernels for 25% -> 24%
where the time goes in v5:
time: 33.6 us; the launch traced here: 33.4 us
  starting transfers between devices  14.1 us (42%)
  Pallas kernels  11.6 us (35%)
  waiting for transfers between devices  7.02 us (21%)
  between operations  0.71 us (2%)
    ppermute x6, starting transfers between devices, swapped(): lax.ppermute(block, axis, [(i, i ^ distance) for i in range(lax.axis_size...  10.4 us
    ppermute x6, waiting for transfers between devices, swapped(): lax.ppermute(block, axis, [(i, i ^ distance) for i in range(lax.axis_size...  6.63 us
    ppermute x4, starting transfers between devices, shifted(): return lax.ppermute(block, axis, route)  3.76 us
    pallas_call x1, Pallas kernels, on_device(): kernel_call(functools.partial(own_kernel, n_head), 'own', shape(feats, ro...  3.41 us
    pallas_call x1, Pallas kernels, on_device(): kernel_call(functools.partial(stage_kernel, n_head), 'stage', [shape(8, H...  2.21 us
    pallas_call x2, Pallas kernels, on_device(): pl.pallas_call(functools.partial(input_sum_kernel, n_other, start), out_s...  1.59 us
    pallas_call x1, Pallas kernels, on_device(): kernel_call(functools.partial(attention_kernel, partners, n_other), 'atte...  1.59 us
    pallas_call x1, Pallas kernels, on_device(): kernel_call(functools.partial(join_kernel, n_copies), 'join', [shape(held...  1.04 us
  transfers between devices with their start and end apart: 10, of which 4 were waited for; matrix products, arithmetic and copies ran while one was open for 0% of the time, Pallas kernels for 24%

profile of v5, /device:TPU:0, one launch (start us, length us, event | category | flops | bytes accessed | tf_op | source)
XLA Modules:
  0.0 33.4 jit_solution(5453558259137177934)
XLA Ops:
  0.6 1.0 %join.1 = (bf16[64,768]{1,0:T(8,128)(2,1)S(1)}, bf16[64,768]{1,0:T(8,128)(2,1)S(1)}, bf16[64,768]{1,0:T(8,128)(2,1)S(1)}, bf16[64,768]{1,0:T(8,128)(2,1)S(1)}, b...) custom-call(bf16[1,64,384]{2,1,0:T(8,128)(2,1)} %key_ref.1, bf16[1,64,384]{2,1,0:T(8,128)(2,1)} %value_ref.1, ...), custom_call_target="tpu_custom_call" | custom-call | tf_op jit(solution)/shard_map/join/pallas_call | solution.py:219
  1.7 3.1 %collective-permute-start = (bf16[64,768]{1,0:T(8,128)(2,1)S(1)}, bf16[64,768]{1,0:T(8,128)(2,1)S(1)}, u32[]{:S(2)}, u32[]{:S(2)}) collective-permute-start(bf16[64,768]{1,0:T(8,128)(2,1)S(1)} %get-tuple-element.25), channel_id=1, source_target_pairs={{0,2},{2,0},{4,6},{6,4},{1,3},{3,1},{5,7},{7,5},{8,10},{10,8},{12,... | collective-permute-start | bytes 294920 | tf_op jit(solution)/shard_map/ppermute | solution.py:26
  4.8 2.6 %collective-permute-start.1 = (bf16[64,768]{1,0:T(8,128)(2,1)S(1)}, bf16[64,768]{1,0:T(8,128)(2,1)S(1)}, u32[]{:S(2)}, u32[]{:S(2)}) collective-permute-start(bf16[64,768]{1,0:T(8,128)(2,1)S(1)} %get-tuple-element.26), channel_id=1, source_target_pairs={{0,4},{2,6},{4,0},{6,2},{1,5},{3,7},{5,1},{7,3},{8,12},{10,14},{12... | collective-permute-start | bytes 294920 | tf_op jit(solution)/shard_map/ppermute | solution.py:26
  7.4 0.4 %collective-permute-start.2 = (bf16[64,768]{1,0:T(8,128)(2,1)S(1)}, bf16[64,768]{1,0:T(8,128)(2,1)S(1)}, u32[]{:S(2)}, u32[]{:S(2)}) collective-permute-start(bf16[64,768]{1,0:T(8,128)(2,1)S(1)} %get-tuple-element.27), channel_id=1, source_target_pairs={{8,0},{16,8},{24,16},{0,24},{9,1},{17,9},{25,17},{1,25},{10,2},{18... | collective-permute-start | bytes 294920 | tf_op jit(solution)/shard_map/ppermute | solution.py:22
  7.7 1.2 %collective-permute-start.3 = (bf16[64,768]{1,0:T(8,128)(2,1)S(1)}, bf16[64,768]{1,0:T(8,128)(2,1)S(1)}, u32[]{:S(2)}, u32[]{:S(2)}) collective-permute-start(bf16[64,768]{1,0:T(8,128)(2,1)S(1)} %get-tuple-element.28), channel_id=1, source_target_pairs={{8,0},{16,8},{24,16},{0,24},{9,1},{17,9},{25,17},{1,25},{10,2},{18... | collective-permute-start | bytes 294920 | tf_op jit(solution)/shard_map/ppermute | solution.py:22
  9.0 0.2 collective-permute-start.4
  9.2 2.2 %stage.1 = (s32[8,128]{1,0:T(8,128)S(1)}, bf16[128,768]{1,0:T(8,128)(2,1)S(1)}, bf16[2688,768]{1,0:T(8,128)(2,1)S(1)}) custom-call(s32[4]{0:T(128)} %span_ref.1, s32[4]{0:T(128)} %prefix_ref.1, bf16[1,128,768]{2,1,0:T(8,128)(2,1)} %q_ref.1, bf16[1,5376,768]{2,1,0:T(8,128)(2,1)} %w_ref.3), custom_call_target="tpu_custom_call" | custom-call | tf_op jit(solution)/shard_map/stage/pallas_call | solution.py:234
  11.4 0.0 collective-permute-done.refs_1_
  11.4 0.9 %collective-permute-done.1.refs_2_ = bf16[64,768]{1,0:T(8,128)(2,1)S(1)} collective-permute-done((bf16[64,768]{1,0:T(8,128)(2,1)S(1)}, bf16[64,768]{1,0:T(8,128)(2,1)S(1)}, u32[]{:S(2)}, u32[]{:S(2)}) %collective-permute-start.1) | collective-permute-done | bytes 98336 | tf_op jit(solution)/shard_map/ppermute | solution.py:26
  12.3 0.0 collective-permute-done.2.refs_3_.d_low
  12.3 0.0 collective-permute-done.3.refs_4_.d_high
  12.3 3.2 %collective-permute-done.4.refs_5_ = bf16[64,768]{1,0:T(8,128)(2,1)S(1)} collective-permute-done((bf16[64,768]{1,0:T(8,128)(2,1)S(1)}, bf16[64,768]{1,0:T(8,128)(2,1)S(1)}, u32[]{:S(2)}, u32[]{:S(2)}) %collective-permute-start.4) | collective-permute-done | bytes 98336 | tf_op jit(solution)/shard_map/ppermute | solution.py:26
  15.5 1.6 %attention.1 = (bf16[768,128]{1,0:T(8,128)(2,1)S(1)}, bf16[3,256,256]{2,1,0:T(8,128)(2,1)S(1)}, bf16[3,256,256]{2,1,0:T(8,128)(2,1)S(1)}, bf16[1424,128]{1,0:T(8,128)(2,1)S(1)}) custom-call(s32[8,128]{1,0:T(8,128)S(1)} %get-tuple-element.22.limit_ref, bf16[128,768]{1,0:T(8,128)(2,1)S(1)} %get-tuple-element.23.q_ref, ...), custom_call_target="tpu_custom_call" | custom-call | tf_op jit(solution)/shard_map/attention/pallas_call | solution.py:249
  17.1 1.6 %collective-permute-start.6 = (bf16[1424,128]{1,0:T(8,128)(2,1)S(1)}, bf16[1424,128]{1,0:T(8,128)(2,1)S(1)}, u32[]{:S(2)}, u32[]{:S(2)}) collective-permute-start(bf16[1424,128]{1,0:T(8,128)(2,1)S(1)} %get-tuple-element.32), channel_id=1, source_target_pairs={{1,0},{0,1},{3,2},{2,3},{5,4},{4,5},{7,6},{6,7},{9,8},{8,9},{11,10... | collective-permute-start | bytes 1093640 | tf_op jit(solution)/shard_map/ppermute | solution.py:22
  18.7 0.7 %rest.1 = bf16[1264,128]{1,0:T(8,128)(2,1)S(1)} custom-call(bf16[768,128]{1,0:T(8,128)(2,1)S(1)} %get-tuple-element.31.grad_ref, bf16[2688,768]{1,0:T(8,128)(2,1)S(1)} %get-tuple-element.30.refs_6_.refs_0_), custom_call_target="tpu_custom_call" | custom-call | tf_op jit(solution)/shard_map/rest/pallas_call | solution.py:255
  19.3 0.6 %collective-permute-start.5 = (bf16[1264,128]{1,0:T(8,128)(2,1)S(1)}, bf16[1264,128]{1,0:T(8,128)(2,1)S(1)}, u32[]{:S(2)}, u32[]{:S(2)}) collective-permute-start(bf16[1264,128]{1,0:T(8,128)(2,1)S(1)} %rest.1), channel_id=1, source_target_pairs={{1,0},{0,1},{3,2},{2,3},{5,4},{4,5},{7,6},{6,7},{9,8},{8,9},{11,10... | collective-permute-start | bytes 970760 | tf_op jit(solution)/shard_map/ppermute | solution.py:22
  19.9 0.4 %terms.1 = (bf16[64,768]{1,0:T(8,128)(2,1)S(1)}, bf16[64,768]{1,0:T(8,128)(2,1)S(1)}, bf16[64,768]{1,0:T(8,128)(2,1)S(1)}, bf16[64,768]{1,0:T(8,128)(2,1)S(1)}) custom-call(bf16[3,256,256]{2,1,0:T(8,128)(2,1)S(1)} %get-tuple-element.33.probs_ref, bf16[3,256,256]{2,1,0:T(8,128)(2,1)S(1)} %get-tuple-element.34.dscores_ref, ...), custom_call_target="tpu_custom_call" | custom-call | tf_op jit(solution)/shard_map/terms/pallas_call | solution.py:262
  20.3 2.2 %collective-permute-start.7 = (bf16[64,768]{1,0:T(8,128)(2,1)S(1)}, bf16[64,768]{1,0:T(8,128)(2,1)S(1)}, u32[]{:S(2)}, u32[]{:S(2)}) collective-permute-start(bf16[64,768]{1,0:T(8,128)(2,1)S(1)} %get-tuple-element.36), channel_id=1, source_target_pairs={{0,6},{2,4},{4,2},{6,0},{1,7},{3,5},{5,3},{7,1},{8,14},{10,12},{12... | collective-permute-start | bytes 294920 | tf_op jit(solution)/shard_map/ppermute | solution.py:26
  22.5 0.7 %collective-permute-start.8 = (bf16[64,768]{1,0:T(8,128)(2,1)S(1)}, bf16[64,768]{1,0:T(8,128)(2,1)S(1)}, u32[]{:S(2)}, u32[]{:S(2)}) collective-permute-start(bf16[64,768]{1,0:T(8,128)(2,1)S(1)} %get-tuple-element.37), channel_id=1, source_target_pairs={{0,4},{2,6},{4,0},{6,2},{1,5},{3,7},{5,1},{7,3},{8,12},{10,14},{12... | collective-permute-start | bytes 294920 | tf_op jit(solution)/shard_map/ppermute | solution.py:26
  23.2 1.6 %collective-permute-start.9 = (bf16[64,768]{1,0:T(8,128)(2,1)S(1)}, bf16[64,768]{1,0:T(8,128)(2,1)S(1)}, u32[]{:S(2)}, u32[]{:S(2)}) collective-permute-start(bf16[64,768]{1,0:T(8,128)(2,1)S(1)} %get-tuple-element.38), channel_id=1, source_target_pairs={{0,2},{2,0},{4,6},{6,4},{1,3},{3,1},{5,7},{7,5},{8,10},{10,8},{12,... | collective-permute-start | bytes 294920 | tf_op jit(solution)/shard_map/ppermute | solution.py:26
  24.7 3.4 %own.1.own_ref = f32[2688,128]{1,0:T(8,128)S(1)} custom-call(bf16[768,128]{1,0:T(8,128)(2,1)S(1)} %get-tuple-element.31.grad_ref, bf16[1,5376,768]{2,1,0:T(8,128)(2,1)} %w_ref.3), custom_call_target="tpu_custom_call" | custom-call | tf_op jit(solution)/shard_map/own/pallas_call | solution.py:271
  28.2 0.0 collective-permute-done.7.refs_1_
  28.2 2.6 %collective-permute-done.8.refs_2_ = bf16[64,768]{1,0:T(8,128)(2,1)S(1)} collective-permute-done((bf16[64,768]{1,0:T(8,128)(2,1)S(1)}, bf16[64,768]{1,0:T(8,128)(2,1)S(1)}, u32[]{:S(2)}, u32[]{:S(2)}) %collective-permute-start.8) | collective-permute-done | bytes 98336 | tf_op jit(solution)/shard_map/ppermute | solution.py:26
  30.7 0.0 collective-permute-done.9.refs_3_
  30.7 0.7 %term_sum.1 = (bf16[1,64,384]{2,1,0:T(8,128)(2,1)}, bf16[1,64,384]{2,1,0:T(8,128)(2,1)}) custom-call(bf16[64,768]{1,0:T(8,128)(2,1)S(1)} %get-tuple-element.35.refs_0_, bf16[64,768]{1,0:T(8,128)(2,1)S(1)} %collective-permute-done.7.refs_1_, bf16[64,768]{1,0:T(8,128)(2,1)S(1)} %collective-permute-done.8.refs_2_, ...), custom_call_target="tpu_custom_call" | custom-call | tf_op jit(solution)/shard_map/term_sum/pallas_call | solution.py:278
  31.4 0.0 collective-permute-done.6.refs_0_
  31.4 0.8 %input_sum.2.refs_1_ = bf16[1,2688,128]{2,1,0:T(8,128)(2,1)} custom-call(f32[2688,128]{1,0:T(8,128)S(1)} %own.1.own_ref, bf16[1424,128]{1,0:T(8,128)(2,1)S(1)} %collective-permute-done.6.refs_0_), custom_call_target="tpu_custom_call" | custom-call | tf_op jit(solution)/shard_map/input_sum/pallas_call | solution.py:284
  32.2 0.4 %collective-permute-done.5.refs_0_ = bf16[1264,128]{1,0:T(8,128)(2,1)S(1)} collective-permute-done((bf16[1264,128]{1,0:T(8,128)(2,1)S(1)}, bf16[1264,128]{1,0:T(8,128)(2,1)S(1)}, u32[]{:S(2)}, u32[]{:S(2)}) %collective-permute-start.5) | collective-permute-done | bytes 323616 | tf_op jit(solution)/shard_map/ppermute | solution.py:22
  32.6 0.8 %input_sum.3 = bf16[1,2688,128]{2,1,0:T(8,128)(2,1)} custom-call(f32[2688,128]{1,0:T(8,128)S(1)} %own.1.own_ref, bf16[1264,128]{1,0:T(8,128)(2,1)S(1)} %collective-permute-done.5.refs_0_, bf16[1,2688,128]{2,1,0:T(8,128)(2,1)} %input_sum.2.refs_1_), custom_call_target="tpu_custom_call", output_to_operand_aliasing={{}: (2, {})} | custom-call | tf_op jit(solution)/shard_map/input_sum/pallas_call | solution.py:284
Async XLA Ops:
  1.7 9.7 %collective-permute-start = (bf16[64,768]{1,0:T(8,128)(2,1)S(1)}, bf16[64,768]{1,0:T(8,128)(2,1)S(1)}, u32[]{:S(2)}, u32[]{:S(2)}) collective-permute-start(bf16[64,768]{1,0:T(8,128)(2,1)S(1)} %get-tuple-element.25), channel_id=1, source_target_pairs={{0,2},{2,0},{4,6},{6,4},{1,3},{3,1},{5,7},{7,5},{8,10},{10,8},{12,... | collective-permute-start | bytes 294920 | tf_op jit(solution)/shard_map/ppermute | solution.py:26
  4.8 7.5 %collective-permute-start.1 = (bf16[64,768]{1,0:T(8,128)(2,1)S(1)}, bf16[64,768]{1,0:T(8,128)(2,1)S(1)}, u32[]{:S(2)}, u32[]{:S(2)}) collective-permute-start(bf16[64,768]{1,0:T(8,128)(2,1)S(1)} %get-tuple-element.26), channel_id=1, source_target_pairs={{0,4},{2,6},{4,0},{6,2},{1,5},{3,7},{5,1},{7,3},{8,12},{10,14},{12... | collective-permute-start | bytes 294920 | tf_op jit(solution)/shard_map/ppermute | solution.py:26
  7.4 5.0 %collective-permute-start.2 = (bf16[64,768]{1,0:T(8,128)(2,1)S(1)}, bf16[64,768]{1,0:T(8,128)(2,1)S(1)}, u32[]{:S(2)}, u32[]{:S(2)}) collective-permute-start(bf16[64,768]{1,0:T(8,128)(2,1)S(1)} %get-tuple-element.27), channel_id=1, source_target_pairs={{8,0},{16,8},{24,16},{0,24},{9,1},{17,9},{25,17},{1,25},{10,2},{18... | collective-permute-start | bytes 294920 | tf_op jit(solution)/shard_map/ppermute | solution.py:22
  7.7 4.6 %collective-permute-start.3 = (bf16[64,768]{1,0:T(8,128)(2,1)S(1)}, bf16[64,768]{1,0:T(8,128)(2,1)S(1)}, u32[]{:S(2)}, u32[]{:S(2)}) collective-permute-start(bf16[64,768]{1,0:T(8,128)(2,1)S(1)} %get-tuple-element.28), channel_id=1, source_target_pairs={{8,0},{16,8},{24,16},{0,24},{9,1},{17,9},{25,17},{1,25},{10,2},{18... | collective-permute-start | bytes 294920 | tf_op jit(solution)/shard_map/ppermute | solution.py:22
  9.0 6.5 %collective-permute-start.4 = (bf16[64,768]{1,0:T(8,128)(2,1)S(1)}, bf16[64,768]{1,0:T(8,128)(2,1)S(1)}, u32[]{:S(2)}, u32[]{:S(2)}) collective-permute-start(bf16[64,768]{1,0:T(8,128)(2,1)S(1)} %get-tuple-element.29), channel_id=1, source_target_pairs={{0,6},{2,4},{4,2},{6,0},{1,7},{3,5},{5,3},{7,1},{8,14},{10,12},{12... | collective-permute-start | bytes 294920 | tf_op jit(solution)/shard_map/ppermute | solution.py:26
  17.1 14.3 %collective-permute-start.6 = (bf16[1424,128]{1,0:T(8,128)(2,1)S(1)}, bf16[1424,128]{1,0:T(8,128)(2,1)S(1)}, u32[]{:S(2)}, u32[]{:S(2)}) collective-permute-start(bf16[1424,128]{1,0:T(8,128)(2,1)S(1)} %get-tuple-element.32), channel_id=1, source_target_pairs={{1,0},{0,1},{3,2},{2,3},{5,4},{4,5},{7,6},{6,7},{9,8},{8,9},{11,10... | collective-permute-start | bytes 1093640 | tf_op jit(solution)/shard_map/ppermute | solution.py:22
  19.3 13.3 %collective-permute-start.5 = (bf16[1264,128]{1,0:T(8,128)(2,1)S(1)}, bf16[1264,128]{1,0:T(8,128)(2,1)S(1)}, u32[]{:S(2)}, u32[]{:S(2)}) collective-permute-start(bf16[1264,128]{1,0:T(8,128)(2,1)S(1)} %rest.1), channel_id=1, source_target_pairs={{1,0},{0,1},{3,2},{2,3},{5,4},{4,5},{7,6},{6,7},{9,8},{8,9},{11,10... | collective-permute-start | bytes 970760 | tf_op jit(solution)/shard_map/ppermute | solution.py:22
  20.3 7.9 %collective-permute-start.7 = (bf16[64,768]{1,0:T(8,128)(2,1)S(1)}, bf16[64,768]{1,0:T(8,128)(2,1)S(1)}, u32[]{:S(2)}, u32[]{:S(2)}) collective-permute-start(bf16[64,768]{1,0:T(8,128)(2,1)S(1)} %get-tuple-element.36), channel_id=1, source_target_pairs={{0,6},{2,4},{4,2},{6,0},{1,7},{3,5},{5,3},{7,1},{8,14},{10,12},{12... | collective-permute-start | bytes 294920 | tf_op jit(solution)/shard_map/ppermute | solution.py:26
  22.5 8.2 %collective-permute-start.8 = (bf16[64,768]{1,0:T(8,128)(2,1)S(1)}, bf16[64,768]{1,0:T(8,128)(2,1)S(1)}, u32[]{:S(2)}, u32[]{:S(2)}) collective-permute-start(bf16[64,768]{1,0:T(8,128)(2,1)S(1)} %get-tuple-element.37), channel_id=1, source_target_pairs={{0,4},{2,6},{4,0},{6,2},{1,5},{3,7},{5,1},{7,3},{8,12},{10,14},{12... | collective-permute-start | bytes 294920 | tf_op jit(solution)/shard_map/ppermute | solution.py:26
  23.2 7.6 %collective-permute-start.9 = (bf16[64,768]{1,0:T(8,128)(2,1)S(1)}, bf16[64,768]{1,0:T(8,128)(2,1)S(1)}, u32[]{:S(2)}, u32[]{:S(2)}) collective-permute-start(bf16[64,768]{1,0:T(8,128)(2,1)S(1)} %get-tuple-element.38), channel_id=1, source_target_pairs={{0,2},{2,0},{4,6},{6,4},{1,3},{3,1},{5,7},{7,5},{8,10},{10,8},{12,... | collective-permute-start | bytes 294920 | tf_op jit(solution)/shard_map/ppermute | solution.py:26
